TPU v7x, 256 devices: a whole 4x4x8 slice. The times are simulated.
256 devices in a mesh: ctx: 64 (over z, x, core), tp: 4 (over y).
Axes of the slice: x: 4, y: 4, z: 8, core: 2. Of those that a mesh axis runs over, the one named last changes fastest.
Arguments:
- queries: bfloat16 [32768, 12, 192], P('ctx', 'tp'), may hold values from -8 to 8
- key_rows: bfloat16 [32768, 192], P('ctx'), may hold values from -8 to 8
- values: bfloat16 [32768, 192], P('ctx'), may hold values from -6 to 6
- grad_out: bfloat16 [32768, 12, 192], P('ctx', 'tp'), may hold values from -6 to 6
- doc_ids: int32 [32768], P('ctx'), may hold values from 0 to 31, never falling along the last dimension, each value on 1 to 2048 neighbouring positions
Outputs:
- attended: bfloat16 [32768, 12, 192], P('ctx', 'tp')
- grad_queries: bfloat16 [32768, 12, 192], P('ctx', 'tp')
- grad_keys: bfloat16 [32768, 192], P(('ctx', 'tp'))
- grad_values: bfloat16 [32768, 192], P(('ctx', 'tp'))
Inputs may be any that keep to these rules, and one draw needn't show every extreme that they name: `doc_ids`: document numbers never fall along the sequence; each document holds 1 to 2048 consecutive tokens, and one holds exactly 2048.
All inputs are finite; a program needn't handle non-finite values.
Results may differ from a plain program's by a relative error of at most 0.018.
Values may be sent and summed in bfloat16 or wider, within the bound.
No kernel may reach another device: no remote copies, remote signals or barrier semaphores. Data moves between devices by JAX's collectives and lax.ppermute only.
A program may use at most 64 MiB of HBM per device.

v0:
```python
import jax
import jax.numpy as jnp
from jax import lax
from jax.sharding import PartitionSpec as P

LOOKBACK = 4


NEGATIVE = -1e30


def from_behind(shard, axis, by):
    size = lax.axis_size(axis)
    pairs = [(i, i + by) for i in range(size) if 0 <= i + by < size]
    return lax.ppermute(shard, axis, pairs)


def head_block(query_part, grad_part, key_window, value_window, visible, scaling):
    scores = jnp.dot(query_part, key_window.T, preferred_element_type=jnp.float32) * scaling
    scores = jnp.where(visible, scores, NEGATIVE)
    highest = jnp.max(scores, axis=-1, keepdims=True)
    exponent = jnp.exp(scores - highest)
    probability = exponent / jnp.sum(exponent, axis=-1, keepdims=True)
    weights = probability.astype(jnp.bfloat16)
    attended = jnp.dot(weights, value_window, preferred_element_type=jnp.float32).astype(
        jnp.bfloat16
    )
    row_delta = jnp.sum(
        grad_part.astype(jnp.float32) * attended.astype(jnp.float32), axis=-1, keepdims=True
    )
    grad_probability = jnp.dot(grad_part, value_window.T, preferred_element_type=jnp.float32)
    grad_scores = (scaling * probability * (grad_probability - row_delta)).astype(jnp.bfloat16)
    grad_query = jnp.dot(grad_scores, key_window, preferred_element_type=jnp.float32).astype(
        jnp.bfloat16
    )
    grad_key = jnp.dot(grad_scores.T, query_part, preferred_element_type=jnp.float32)
    grad_value = jnp.dot(weights.T, grad_part, preferred_element_type=jnp.float32)
    return (attended, grad_query, grad_key, grad_value)


def local(queries, key_rows, values, grad_out, doc_ids):
    row_count = queries.shape[0]
    head_count = queries.shape[1]
    head_dim = queries.shape[2]
    reach = LOOKBACK
    raised_docs = doc_ids + 1
    earlier_docs = [from_behind(raised_docs, "ctx", offset) - 1 for offset in range(reach, 0, -1)]
    key_docs = jnp.concatenate(earlier_docs + [doc_ids], axis=0)
    paired = jnp.stack([key_rows, values])
    earlier = [from_behind(paired, "ctx", offset) for offset in range(reach, 0, -1)]
    window = jnp.concatenate(earlier + [paired], axis=1)
    key_window = window[0]
    value_window = window[1]
    span_rows = reach * row_count
    query_places = jnp.arange(row_count, dtype=jnp.int32) + span_rows
    key_places = jnp.arange(span_rows + row_count, dtype=jnp.int32)
    scaling = head_dim ** (-0.5)
    block_rows = min(512, row_count)
    key_grads = jnp.zeros((span_rows + row_count, head_dim), jnp.float32)
    value_grads = jnp.zeros((span_rows + row_count, head_dim), jnp.float32)
    attended_heads = []
    grad_heads_list = []
    for head_index in range(head_count):
        visible = (doc_ids[0:block_rows, None] == key_docs[None, :]) & (
            key_places[None, :] <= query_places[0:block_rows, None]
        )
        attended, grad_query, grad_key, grad_value = head_block(
            queries[0:block_rows, head_index],
            grad_out[0:block_rows, head_index],
            key_window,
            value_window,
            visible,
            scaling,
        )
        key_grads = key_grads + grad_key
        value_grads = value_grads + grad_value
        attended_heads.append(attended)
        grad_heads_list.append(grad_query)
    attended_all = jnp.stack(attended_heads, axis=1)
    grad_queries = jnp.stack(grad_heads_list, axis=1)
    both_grads = jnp.stack([key_grads, value_grads])
    tile_grads = [
        both_grads[:, tile_index * row_count : (tile_index + 1) * row_count]
        for tile_index in range(reach + 1)
    ]
    summed_grads = tile_grads[reach]
    for tile_index in range(reach):
        summed_grads = summed_grads + from_behind(
            tile_grads[tile_index].astype(jnp.bfloat16), "ctx", tile_index - reach
        ).astype(jnp.float32)
    own_grads = lax.psum_scatter(
        summed_grads.astype(jnp.bfloat16), "tp", scatter_dimension=1, tiled=True
    ).astype(jnp.float32)
    return (
        attended_all,
        grad_queries,
        own_grads[0].astype(jnp.bfloat16),
        own_grads[1].astype(jnp.bfloat16),
    )


def solution(mesh):
    placed = (P("ctx", "tp", None), P("ctx", None), P("ctx", None), P("ctx", "tp", None), P("ctx"))
    return jax.shard_map(
        local,
        mesh=mesh,
        in_specs=placed,
        out_specs=(
            P("ctx", "tp", None),
            P("ctx", "tp", None),
            P(("ctx", "tp"), None),
            P(("ctx", "tp"), None),
        ),
        check_vma=False,
    )
```

profile of v0, /device:TPU:102, one launch (start us, length us, event | category | flops | bytes accessed | tf_op | source)
XLA Modules:
  0.0 163.6 jit_solution(12615115799239656433)
XLA Ops:
  7.3 1.2 pad_maximum_fusion.3
  8.4 5.9 %collective-permute-start.4 = (bf16[2,512,192]{1,2,0:T(8,128)(2,1)S(1)}, bf16[2,512,192]{1,2,0:T(8,128)(2,1)S(1)}, u32[]{:S(2)}, u32[]{:S(2)}) collective-permute-start(bf16[2,512,192]{1,2,0:T(8,128)(2,1)S(1)} %pad_maximum_fusion.3), channel_id=1, source_target_pairs={{0,16},{4,20},{8,24},{12,28},{16,32},{20,36},{24,40},{28,44},{32,4... | collective-permute-start | bytes 1179656 | tf_op jit(solution)/shard_map/ppermute | solution.py:15
  14.3 3.2 %collective-permute-start.5 = (bf16[2,512,192]{1,2,0:T(8,128)(2,1)S(1)}, bf16[2,512,192]{1,2,0:T(8,128)(2,1)S(1)}, u32[]{:S(2)}, u32[]{:S(2)}) collective-permute-start(bf16[2,512,192]{1,2,0:T(8,128)(2,1)S(1)} %pad_maximum_fusion.3), channel_id=1, source_target_pairs={{0,12},{4,16},{8,20},{12,24},{16,28},{20,32},{24,36},{28,40},{32,4... | collective-permute-start | bytes 1179656 | tf_op jit(solution)/shard_map/ppermute | solution.py:15
  17.5 2.8 %collective-permute-start.6 = (bf16[2,512,192]{1,2,0:T(8,128)(2,1)S(1)}, bf16[2,512,192]{1,2,0:T(8,128)(2,1)S(1)}, u32[]{:S(2)}, u32[]{:S(2)}) collective-permute-start(bf16[2,512,192]{1,2,0:T(8,128)(2,1)S(1)} %pad_maximum_fusion.3), channel_id=1, source_target_pairs={{0,8},{4,12},{8,16},{12,20},{16,24},{20,28},{24,32},{28,36},{32,40... | collective-permute-start | bytes 1179656 | tf_op jit(solution)/shard_map/ppermute | solution.py:15
  20.3 2.7 %collective-permute-start.7 = (bf16[2,512,192]{1,2,0:T(8,128)(2,1)S(1)}, bf16[2,512,192]{1,2,0:T(8,128)(2,1)S(1)}, u32[]{:S(2)}, u32[]{:S(2)}) collective-permute-start(bf16[2,512,192]{1,2,0:T(8,128)(2,1)S(1)} %pad_maximum_fusion.3), channel_id=1, source_target_pairs={{0,4},{4,8},{8,12},{12,16},{16,20},{20,24},{24,28},{28,32},{32,36}... | collective-permute-start | bytes 1179656 | tf_op jit(solution)/shard_map/ppermute | solution.py:15
  23.0 0.7 broadcast_add_fusion
  23.7 4.3 %collective-permute-start = (s32[512]{0:T(512)S(1)}, s32[512]{0:T(512)S(1)}, u32[]{:S(2)}, u32[]{:S(2)}) collective-permute-start(s32[512]{0:T(512)S(1)} %broadcast_add_fusion), channel_id=1, source_target_pairs={{0,16},{4,20},{8,24},{12,28},{16,32},{20,36},{24,40},{28,44},{32,4... | collective-permute-start | bytes 6152 | tf_op jit(solution)/shard_map/ppermute | solution.py:15
  28.0 12.7 %collective-permute-done = s32[512]{0:T(512)S(1)} collective-permute-done((s32[512]{0:T(512)S(1)}, s32[512]{0:T(512)S(1)}, u32[]{:S(2)}, u32[]{:S(2)}) %collective-permute-start) | collective-permute-done | bytes 2080 | tf_op jit(solution)/shard_map/ppermute | solution.py:15
  40.7 6.8 %collective-permute-start.1 = (s32[512]{0:T(512)S(1)}, s32[512]{0:T(512)S(1)}, u32[]{:S(2)}, u32[]{:S(2)}) collective-permute-start(s32[512]{0:T(512)S(1)} %broadcast_add_fusion), channel_id=1, source_target_pairs={{0,12},{4,16},{8,20},{12,24},{16,28},{20,32},{24,36},{28,40},{32,4... | collective-permute-start | bytes 6152 | tf_op jit(solution)/shard_map/ppermute | solution.py:15
  47.6 1.3 collective-permute-done.1
  48.8 6.1 %collective-permute-start.2 = (s32[512]{0:T(512)S(1)}, s32[512]{0:T(512)S(1)}, u32[]{:S(2)}, u32[]{:S(2)}) collective-permute-start(s32[512]{0:T(512)S(1)} %broadcast_add_fusion), channel_id=1, source_target_pairs={{0,8},{4,12},{8,16},{12,20},{16,24},{20,28},{24,32},{28,36},{32,40... | collective-permute-start | bytes 6152 | tf_op jit(solution)/shard_map/ppermute | solution.py:15
  55.0 1.3 collective-permute-done.2
  56.3 2.2 %collective-permute-start.3 = (s32[512]{0:T(512)S(1)}, s32[512]{0:T(512)S(1)}, u32[]{:S(2)}, u32[]{:S(2)}) collective-permute-start(s32[512]{0:T(512)S(1)} %broadcast_add_fusion), channel_id=1, source_target_pairs={{0,4},{4,8},{8,12},{12,16},{16,20},{20,24},{24,28},{28,32},{32,36}... | collective-permute-start | bytes 6152 | tf_op jit(solution)/shard_map/ppermute | solution.py:15
  58.5 2.6 %collective-permute-done.3 = s32[512]{0:T(512)S(1)} collective-permute-done((s32[512]{0:T(512)S(1)}, s32[512]{0:T(512)S(1)}, u32[]{:S(2)}, u32[]{:S(2)}) %collective-permute-start.3) | collective-permute-done | bytes 2080 | tf_op jit(solution)/shard_map/ppermute | solution.py:15
  61.2 0.7 constant_dynamic-update-slice_fusion.6
  62.1 1.6 fusion.55
  63.7 1.6 fusion.54
  65.3 1.6 fusion.53
  66.9 0.8 fusion.5
  67.6 0.9 fusion.15
  68.5 0.8 fusion.7
  69.3 0.9 fusion.14
  71.3 1.0 fusion.29
  72.3 1.0 convolution_add_fusion.1
  73.3 0.8 fusion.9
  74.0 0.9 fusion.13
  75.6 1.2 fusion.12
  76.8 1.4 multiply_reduce_fusion.2
  78.2 1.5 fusion.2
  79.7 1.0 fusion.36
  81.2 1.5 fusion.1
  82.8 1.5 fusion
  84.3 1.0 convolution_add_fusion.3
  85.4 1.0 fusion.11
  86.9 1.9 %collective-permute-start.10 = (bf16[2,512,192]{1,2,0:T(8,128)(2,1)S(1)}, bf16[2,512,192]{1,2,0:T(8,128)(2,1)S(1)}, u32[]{:S(2)}, u32[]{:S(2)}) collective-permute-start(bf16[2,512,192]{1,2,0:T(8,128)(2,1)S(1)} %get-tuple-element.9), channel_id=1, source_target_pairs={{8,0},{12,4},{16,8},{20,12},{24,16},{28,20},{32,24},{36,28},{40,32... | collective-permute-start | bytes 1179656 | tf_op jit(solution)/shard_map/ppermute | solution.py:15
  88.8 1.9 %collective-permute-start.11 = (bf16[2,512,192]{1,2,0:T(8,128)(2,1)S(1)}, bf16[2,512,192]{1,2,0:T(8,128)(2,1)S(1)}, u32[]{:S(2)}, u32[]{:S(2)}) collective-permute-start(bf16[2,512,192]{1,2,0:T(8,128)(2,1)S(1)} %get-tuple-element.8), channel_id=1, source_target_pairs={{4,0},{8,4},{12,8},{16,12},{20,16},{24,20},{28,24},{32,28},{36,32}... | collective-permute-start | bytes 1179656 | tf_op jit(solution)/shard_map/ppermute | solution.py:15
  90.8 6.3 %collective-permute-start.8 = (bf16[2,512,192]{1,2,0:T(8,128)(2,1)S(1)}, bf16[2,512,192]{1,2,0:T(8,128)(2,1)S(1)}, u32[]{:S(2)}, u32[]{:S(2)}) collective-permute-start(bf16[2,512,192]{1,2,0:T(8,128)(2,1)S(1)} %get-tuple-element.7), channel_id=1, source_target_pairs={{16,0},{20,4},{24,8},{28,12},{32,16},{36,20},{40,24},{44,28},{48,3... | collective-permute-start | bytes 1179656 | tf_op jit(solution)/shard_map/ppermute | solution.py:15
  97.0 2.0 %collective-permute-start.9 = (bf16[2,512,192]{1,2,0:T(8,128)(2,1)S(1)}, bf16[2,512,192]{1,2,0:T(8,128)(2,1)S(1)}, u32[]{:S(2)}, u32[]{:S(2)}) collective-permute-start(bf16[2,512,192]{1,2,0:T(8,128)(2,1)S(1)} %get-tuple-element.10), channel_id=1, source_target_pairs={{12,0},{16,4},{20,8},{24,12},{28,16},{32,20},{36,24},{40,28},{44,3... | collective-permute-start | bytes 1179656 | tf_op jit(solution)/shard_map/ppermute | solution.py:15
  99.1 10.1 %collective-permute-done.10 = bf16[2,512,192]{1,2,0:T(8,128)(2,1)S(1)} collective-permute-done((bf16[2,512,192]{1,2,0:T(8,128)(2,1)S(1)}, bf16[2,512,192]{1,2,0:T(8,128)(2,1)S(1)}, u32[]{:S(2)}, u32[]{:S(2)}) %collective-permute-start.10) | collective-permute-done | bytes 393248 | tf_op jit(solution)/shard_map/ppermute | solution.py:15
  109.2 11.4 %collective-permute-done.8 = bf16[2,512,192]{1,2,0:T(8,128)(2,1)S(1)} collective-permute-done((bf16[2,512,192]{1,2,0:T(8,128)(2,1)S(1)}, bf16[2,512,192]{1,2,0:T(8,128)(2,1)S(1)}, u32[]{:S(2)}, u32[]{:S(2)}) %collective-permute-start.8) | collective-permute-done | bytes 393248 | tf_op jit(solution)/shard_map/ppermute | solution.py:15
  120.5 5.8 %collective-permute-done.9 = bf16[2,512,192]{1,2,0:T(8,128)(2,1)S(1)} collective-permute-done((bf16[2,512,192]{1,2,0:T(8,128)(2,1)S(1)}, bf16[2,512,192]{1,2,0:T(8,128)(2,1)S(1)}, u32[]{:S(2)}, u32[]{:S(2)}) %collective-permute-start.9) | collective-permute-done | bytes 393248 | tf_op jit(solution)/shard_map/ppermute | solution.py:15
  127.1 1.0 reshape.25
  128.1 2.9 %fusion.16 = bf16[512,1,192]{0,2,1:T(8,128)(2,1)S(1)} fusion(bf16[512,2560]{0,1:T(8,128)(2,1)} %copy-done.2, bf16[2,2560,192]{1,2,0:T(8,128)(2,1)} %copy-done.12), kind=kOutput, calls=%fused_computation.39 | convolution fusion | flops 503414784 | bytes 3801088 | tf_op jit(solution)/shard_map/dot_general | solution.py:33
  133.3 1.1 pad_maximum_fusion.1
  134.5 19.5 %reduce-scatter.4.cloned.1.call-done = bf16[128,384]{1,0:T(8,128)(2,1)} async-done(((bf16[512,384]{1,0:T(8,128)(2,1)}), bf16[128,384]{1,0:T(8,128)(2,1)}) %reduce-scatter.4.cloned.1.call-update) | async-done | bytes 98320
  154.0 1.0 reshape.26
  155.2 0.7 copy.11
  156.0 0.7 copy.12
  (57 shorter events, 6.2 us)
Async XLA Ops:
  7.2 54.8 %copy-start.4 = (bf16[512,192]{0,1:T(8,128)(2,1)S(1)}, bf16[512,192]{0,1:T(8,128)(2,1)}, u32[]{:S(2)}) copy-start(bf16[512,192]{0,1:T(8,128)(2,1)} %param.6) | copy-start | bytes 589828
  7.2 54.8 %copy-start.3 = (bf16[512,192]{0,1:T(8,128)(2,1)S(1)}, bf16[512,192]{0,1:T(8,128)(2,1)}, u32[]{:S(2)}) copy-start(bf16[512,192]{0,1:T(8,128)(2,1)} %param.7) | copy-start | bytes 589828
  7.2 54.9 %copy-start.14 = (s32[512]{0:T(512)S(1)}, s32[512]{0:T(512)}, u32[]{:S(2)}) copy-start(s32[512]{0:T(512)} %param.9) | copy-start | bytes 6148
  7.2 54.9 %copy-start.6 = (bf16[512,3,192]{0,2,1:T(8,128)(2,1)S(1)}, bf16[512,3,192]{0,2,1:T(8,128)(2,1)}, u32[]{:S(2)}) copy-start(bf16[512,3,192]{0,2,1:T(8,128)(2,1)} %param.5) | copy-start | bytes 1769476
  7.2 146.8 %reduce-scatter.4.cloned.1.call-start = ((), (), s32[]{:S(2)}) async-start(), calls=%async_computation.1 | async-start | bytes 491520
  8.4 53.4 %collective-permute-start.4 = (bf16[2,512,192]{1,2,0:T(8,128)(2,1)S(1)}, bf16[2,512,192]{1,2,0:T(8,128)(2,1)S(1)}, u32[]{:S(2)}, u32[]{:S(2)}) collective-permute-start(bf16[2,512,192]{1,2,0:T(8,128)(2,1)S(1)} %pad_maximum_fusion.3), channel_id=1, source_target_pairs={{0,16},{4,20},{8,24},{12,28},{16,32},{20,36},{24,40},{28,44},{32,4... | collective-permute-start | bytes 1179656 | tf_op jit(solution)/shard_map/ppermute | solution.py:15
  14.3 47.5 %collective-permute-start.5 = (bf16[2,512,192]{1,2,0:T(8,128)(2,1)S(1)}, bf16[2,512,192]{1,2,0:T(8,128)(2,1)S(1)}, u32[]{:S(2)}, u32[]{:S(2)}) collective-permute-start(bf16[2,512,192]{1,2,0:T(8,128)(2,1)S(1)} %pad_maximum_fusion.3), channel_id=1, source_target_pairs={{0,12},{4,16},{8,20},{12,24},{16,28},{20,32},{24,36},{28,40},{32,4... | collective-permute-start | bytes 1179656 | tf_op jit(solution)/shard_map/ppermute | solution.py:15
  17.5 44.4 %collective-permute-start.6 = (bf16[2,512,192]{1,2,0:T(8,128)(2,1)S(1)}, bf16[2,512,192]{1,2,0:T(8,128)(2,1)S(1)}, u32[]{:S(2)}, u32[]{:S(2)}) collective-permute-start(bf16[2,512,192]{1,2,0:T(8,128)(2,1)S(1)} %pad_maximum_fusion.3), channel_id=1, source_target_pairs={{0,8},{4,12},{8,16},{12,20},{16,24},{20,28},{24,32},{28,36},{32,40... | collective-permute-start | bytes 1179656 | tf_op jit(solution)/shard_map/ppermute | solution.py:15
  20.3 41.7 %collective-permute-start.7 = (bf16[2,512,192]{1,2,0:T(8,128)(2,1)S(1)}, bf16[2,512,192]{1,2,0:T(8,128)(2,1)S(1)}, u32[]{:S(2)}, u32[]{:S(2)}) collective-permute-start(bf16[2,512,192]{1,2,0:T(8,128)(2,1)S(1)} %pad_maximum_fusion.3), channel_id=1, source_target_pairs={{0,4},{4,8},{8,12},{12,16},{16,20},{20,24},{24,28},{28,32},{32,36}... | collective-permute-start | bytes 1179656 | tf_op jit(solution)/shard_map/ppermute | solution.py:15
  23.7 17.1 %collective-permute-start = (s32[512]{0:T(512)S(1)}, s32[512]{0:T(512)S(1)}, u32[]{:S(2)}, u32[]{:S(2)}) collective-permute-start(s32[512]{0:T(512)S(1)} %broadcast_add_fusion), channel_id=1, source_target_pairs={{0,16},{4,20},{8,24},{12,28},{16,32},{20,36},{24,40},{28,44},{32,4... | collective-permute-start | bytes 6152 | tf_op jit(solution)/shard_map/ppermute | solution.py:15
  40.7 8.1 %collective-permute-start.1 = (s32[512]{0:T(512)S(1)}, s32[512]{0:T(512)S(1)}, u32[]{:S(2)}, u32[]{:S(2)}) collective-permute-start(s32[512]{0:T(512)S(1)} %broadcast_add_fusion), channel_id=1, source_target_pairs={{0,12},{4,16},{8,20},{12,24},{16,28},{20,32},{24,36},{28,40},{32,4... | collective-permute-start | bytes 6152 | tf_op jit(solution)/shard_map/ppermute | solution.py:15
  48.8 7.4 %collective-permute-start.2 = (s32[512]{0:T(512)S(1)}, s32[512]{0:T(512)S(1)}, u32[]{:S(2)}, u32[]{:S(2)}) collective-permute-start(s32[512]{0:T(512)S(1)} %broadcast_add_fusion), channel_id=1, source_target_pairs={{0,8},{4,12},{8,16},{12,20},{16,24},{20,28},{24,32},{28,36},{32,40... | collective-permute-start | bytes 6152 | tf_op jit(solution)/shard_map/ppermute | solution.py:15
  56.3 4.9 %collective-permute-start.3 = (s32[512]{0:T(512)S(1)}, s32[512]{0:T(512)S(1)}, u32[]{:S(2)}, u32[]{:S(2)}) collective-permute-start(s32[512]{0:T(512)S(1)} %broadcast_add_fusion), channel_id=1, source_target_pairs={{0,4},{4,8},{8,12},{12,16},{16,20},{20,24},{24,28},{28,32},{32,36}... | collective-permute-start | bytes 6152 | tf_op jit(solution)/shard_map/ppermute | solution.py:15
  62.1 20.7 %copy-start.12 = (bf16[2,2560,192]{1,2,0:T(8,128)(2,1)}, bf16[2,2560,192]{1,2,0:T(8,128)(2,1)S(1)}, u32[]{:S(2)}) copy-start(bf16[2,2560,192]{1,2,0:T(8,128)(2,1)S(1)} %constant_dynamic-update-slice_fusion) | copy-start | bytes 5898244
  70.2 1.1 copy-start.5
  71.3 5.5 %copy-start.7 = (bf16[512,192]{0,1:T(8,128)(2,1)}, bf16[512,192]{0,1:T(8,128)(2,1)S(1)}, u32[]{:S(2)}) copy-start(bf16[512,192]{0,1:T(8,128)(2,1)S(1)} %convolution_convert_fusion.4) | copy-start | bytes 589828
  75.6 1.2 copy-start.9
  79.7 1.5 copy-start.2
  82.7 1.6 copy-start
  86.9 22.2 %collective-permute-start.10 = (bf16[2,512,192]{1,2,0:T(8,128)(2,1)S(1)}, bf16[2,512,192]{1,2,0:T(8,128)(2,1)S(1)}, u32[]{:S(2)}, u32[]{:S(2)}) collective-permute-start(bf16[2,512,192]{1,2,0:T(8,128)(2,1)S(1)} %get-tuple-element.9), channel_id=1, source_target_pairs={{8,0},{12,4},{16,8},{20,12},{24,16},{28,20},{32,24},{36,28},{40,32... | collective-permute-start | bytes 1179656 | tf_op jit(solution)/shard_map/ppermute | solution.py:15
  88.8 20.3 %collective-permute-start.11 = (bf16[2,512,192]{1,2,0:T(8,128)(2,1)S(1)}, bf16[2,512,192]{1,2,0:T(8,128)(2,1)S(1)}, u32[]{:S(2)}, u32[]{:S(2)}) collective-permute-start(bf16[2,512,192]{1,2,0:T(8,128)(2,1)S(1)} %get-tuple-element.8), channel_id=1, source_target_pairs={{4,0},{8,4},{12,8},{16,12},{20,16},{24,20},{28,24},{32,28},{36,32}... | collective-permute-start | bytes 1179656 | tf_op jit(solution)/shard_map/ppermute | solution.py:15
  90.8 29.8 %collective-permute-start.8 = (bf16[2,512,192]{1,2,0:T(8,128)(2,1)S(1)}, bf16[2,512,192]{1,2,0:T(8,128)(2,1)S(1)}, u32[]{:S(2)}, u32[]{:S(2)}) collective-permute-start(bf16[2,512,192]{1,2,0:T(8,128)(2,1)S(1)} %get-tuple-element.7), channel_id=1, source_target_pairs={{16,0},{20,4},{24,8},{28,12},{32,16},{36,20},{40,24},{44,28},{48,3... | collective-permute-start | bytes 1179656 | tf_op jit(solution)/shard_map/ppermute | solution.py:15
  97.0 29.3 %collective-permute-start.9 = (bf16[2,512,192]{1,2,0:T(8,128)(2,1)S(1)}, bf16[2,512,192]{1,2,0:T(8,128)(2,1)S(1)}, u32[]{:S(2)}, u32[]{:S(2)}) collective-permute-start(bf16[2,512,192]{1,2,0:T(8,128)(2,1)S(1)} %get-tuple-element.10), channel_id=1, source_target_pairs={{12,0},{16,4},{20,8},{24,12},{28,16},{32,20},{36,24},{40,28},{44,3... | collective-permute-start | bytes 1179656 | tf_op jit(solution)/shard_map/ppermute | solution.py:15
  128.1 2.9 %copy-start.1 = (bf16[512,2560]{0,1:T(8,128)(2,1)S(1)}, bf16[512,2560]{0,1:T(8,128)(2,1)}, u32[]{:S(2)}) copy-start(bf16[512,2560]{0,1:T(8,128)(2,1)} %copy-done) | copy-start | bytes 7864324
  128.1 3.4 %copy-start.13 = (bf16[2,2560,192]{1,2,0:T(8,128)(2,1)S(1)}, bf16[2,2560,192]{1,2,0:T(8,128)(2,1)}, u32[]{:S(2)}) copy-start(bf16[2,2560,192]{1,2,0:T(8,128)(2,1)} %copy-done.12) | copy-start | bytes 5898244
  132.2 0.9 copy-start.8
  132.2 1.0 copy-start.10
  132.3 1.1 copy-start.11
Sparse Core Ops, SparseCore 0:
  128.2 25.7 reduce-scatter.3
where the time goes:
time: 165 us; the launch traced here: 164 us
  waiting for transfers between devices  64.7 us (39%)
  starting transfers between devices  46.2 us (28%)
  matrix products  22.5 us (14%)
  between operations  14.6 us (9%)
  other arithmetic  8.68 us (5%)
  local copies, waits for them, and re-layouts  6.94 us (4%)
    ppermute x12, starting transfers between devices, from_behind(): return lax.ppermute(shard, axis, pairs)  46.1 us
    ppermute x12, waiting for transfers between devices, from_behind(): return lax.ppermute(shard, axis, pairs)  45.2 us
    unnamed x2, waiting for transfers between devices  19.6 us
    unnamed x39, local copies, waits for them, and re-layouts  5.92 us
    dot_general x3, matrix products, head_block(): jnp.dot(query_part, key_window.T, preferred_element_type=jnp.float32)  4.77 us
    dot_general x3, matrix products, head_block(): jnp.dot(grad_part, value_window.T, preferred_element_type=jnp.float32)  4.57 us
    dot_general x3, matrix products, head_block(): jnp.dot(grad_scores, key_window, preferred_element_type=jnp.float32)  4.2 us
  transfers between devices with their start and end apart: 13, of which 8 were waited for; matrix products, arithmetic and copies ran while one was open for 4% of the time, Pallas kernels for 0%

commit v1 on v0

v1 whole, which is shorter than its diff:
```python
import jax
import jax.numpy as jnp
from jax import lax
from jax.experimental import pallas as pl
from jax.experimental.pallas import tpu as pltpu
from jax.sharding import PartitionSpec as P

LOG2E = 1.4426950408889634
NEGATIVE = -1e30
ROWS = 512
CHUNK = 256
PIECE = 128
DIM = 192
DOC_ROW = 2 * DIM
PACKED = DOC_ROW + 16
REMOTE_CHUNKS = 8
HEADS = 3
COLS = HEADS * ROWS
OFFSETS = (0, 3, 1, 2)
F32 = jnp.float32
BF16 = jnp.bfloat16


def dot(a, b):
    return jnp.dot(a, b, preferred_element_type=F32)


def one_hot(docs, width):
    rows = lax.broadcasted_iota(jnp.int32, (64, width), 0).astype(F32)
    return rows == docs.astype(F32)


def attention_kernel(
    tp_ref, q_ref, do_ref, own_ref, g0_ref, g1_ref, g2_ref, g3_ref, sw_ref,
    o_ref, dq_ref, dkv_ref,
    kt, vt, kn, vn, scores, weights, ds_ref, qe, qn, dop, don, top, total, oacc, dqacc,
):
    tp = tp_ref[0]
    gathered = (g0_ref, g1_ref, g2_ref, g3_ref)
    scale = DIM ** -0.5
    to_log2 = scale * LOG2E

    def piece_of(tile, slot):
        if tile % 2 == 0:
            return gathered[slot].at[tile // 2]
        return sw_ref.at[slot, tile // 2]

    own_docs = own_ref[DOC_ROW : DOC_ROW + 1, :].astype(F32)
    first_doc = own_docs[:, 0:1]
    matches = jnp.zeros((1, PIECE), F32)
    for tile in range(4):
        for slot in range(4):
            docs = piece_of(tile, slot)[DOC_ROW : DOC_ROW + 1, :].astype(F32)
            matches = matches + jnp.where(docs == first_doc, 1.0, 0.0)
    reach = jnp.sum(matches).astype(jnp.int32)
    first_chunk = (REMOTE_CHUNKS * CHUNK - reach) // CHUNK

    def place(chunk, lanes, rows, piece):
        width = piece.shape[1]
        keys = piece[0:DIM, :]
        vals = piece[DIM : 2 * DIM, :]
        kt[chunk, :, lanes] = keys
        vt[chunk, :, lanes] = vals
        hot = one_hot(piece[DOC_ROW : DOC_ROW + 1, :], width).astype(F32).astype(BF16)
        kn[chunk, rows, :] = jnp.concatenate([keys, hot], axis=0).T
        vn[chunk, rows, :] = vals.T

    for tile in range(4):
        for slot in range(4):
            quarter = lax.rem(tp + OFFSETS[slot], 4)
            chunk = tile * 2 + quarter // 2
            half = lax.rem(quarter, 2) * PIECE

            @pl.when(chunk >= first_chunk)
            def _():
                span = pl.ds(pl.multiple_of(half, PIECE), PIECE)
                place(chunk, span, span, piece_of(tile, slot)[...])

    for part in range(2):
        span = slice(part * CHUNK, (part + 1) * CHUNK)
        place(REMOTE_CHUNKS + part, slice(None), slice(None), own_ref[:, span])

    mask_rows = jnp.where(one_hot(own_docs, ROWS), 0.0, NEGATIVE).astype(BF16)
    for head in range(HEADS):
        cols = slice(head * ROWS, (head + 1) * ROWS)
        qe[0:DIM, cols] = q_ref[head]
        qe[DIM:, cols] = mask_rows
        qn[cols, :] = q_ref[head].T

    causal = lax.broadcasted_iota(jnp.int32, (CHUNK, CHUNK), 0) <= lax.broadcasted_iota(
        jnp.int32, (CHUNK, CHUNK), 1
    )

    def highest(s):
        return jnp.max(s.reshape(CHUNK // 8, 8, s.shape[1]), axis=0)

    for head in range(HEADS):
        low = slice(head * ROWS, head * ROWS + CHUNK)
        high = slice(head * ROWS + CHUNK, (head + 1) * ROWS)
        s_low = jnp.where(causal, dot(kn[REMOTE_CHUNKS], qe[:, low]), NEGATIVE)
        s_high = dot(kn[REMOTE_CHUNKS], qe[:, high])
        s_last = jnp.where(causal, dot(kn[REMOTE_CHUNKS + 1], qe[:, high]), NEGATIVE)
        scores[REMOTE_CHUNKS, :, low] = s_low
        scores[REMOTE_CHUNKS, :, high] = s_high
        scores[REMOTE_CHUNKS + 1, :, high] = s_last
        top[:, low] = highest(s_low)
        top[:, high] = jnp.maximum(highest(s_high), highest(s_last))

    @pl.loop(first_chunk, REMOTE_CHUNKS)
    def _(chunk):
        for head in range(HEADS):
            cols = slice(head * ROWS, (head + 1) * ROWS)
            s = dot(kn[chunk], qe[:, cols])
            scores[chunk, :, cols] = s
            top[:, cols] = jnp.maximum(top[:, cols], highest(s))

    top[...] = jnp.broadcast_to(jnp.max(top[...], axis=0, keepdims=True) * to_log2, (8, COLS))

    def exponent(chunk, cols):
        width = cols.stop - cols.start
        s = scores[chunk, :, cols].reshape(CHUNK // 8, 8, width)
        e = jnp.exp2(s * to_log2 - top[:, cols][None])
        part = jnp.sum(e, axis=0)
        w = e.reshape(CHUNK, width).astype(BF16)
        weights[chunk, :, cols] = w
        return part, w

    for head in range(HEADS):
        cols = slice(head * ROWS, (head + 1) * ROWS)
        high = slice(head * ROWS + CHUNK, (head + 1) * ROWS)
        part, w = exponent(REMOTE_CHUNKS, cols)
        total[:, cols] = part
        oacc[:, cols] = dot(vt[REMOTE_CHUNKS], w)
        part, w = exponent(REMOTE_CHUNKS + 1, high)
        total[:, high] += part
        oacc[:, high] += dot(vt[REMOTE_CHUNKS + 1], w)

    @pl.loop(first_chunk, REMOTE_CHUNKS)
    def _(chunk):
        for head in range(HEADS):
            cols = slice(head * ROWS, (head + 1) * ROWS)
            part, w = exponent(chunk, cols)
            total[:, cols] += part
            oacc[:, cols] += dot(vt[chunk], w)

    for head in range(HEADS):
        cols = slice(head * ROWS, (head + 1) * ROWS)
        inverse = 1.0 / jnp.sum(total[:, cols], axis=0, keepdims=True)
        attended = (oacc[:, cols] * inverse).astype(BF16)
        o_ref[head] = attended
        grads = do_ref[head].astype(F32)
        delta = jnp.sum(grads * attended.astype(F32), axis=0, keepdims=True)
        ratio = inverse * scale
        top[:, cols] = jnp.broadcast_to(delta * ratio, (8, ROWS))
        scaled = (grads * ratio).astype(BF16)
        dop[:, cols] = scaled
        don[cols, :] = scaled.T

    def grad_scores(chunk, cols):
        width = cols.stop - cols.start
        dp = dot(vn[chunk], dop[:, cols]).reshape(CHUNK // 8, 8, width)
        w = weights[chunk, :, cols].astype(F32).reshape(CHUNK // 8, 8, width)
        ds = (w * (dp - top[:, cols][None])).reshape(CHUNK, width).astype(BF16)
        ds_ref[:, cols] = ds
        return ds

    def emit(chunk, dk, dv):
        both = jnp.concatenate([dk, dv * (1.0 / scale)], axis=1).astype(BF16)
        for half in range(2):
            quarter = lax.rem(chunk, 2) * 2 + half
            off = lax.rem(quarter - tp + 4, 4)
            slot = jnp.where(off == 0, 0, jnp.where(off == 3, 1, off + 1))
            dkv_ref[chunk // 2, slot] = both[half * PIECE : (half + 1) * PIECE]

    for part in range(2):
        chunk = REMOTE_CHUNKS + part
        dk = jnp.zeros((CHUNK, DIM), F32)
        dv = jnp.zeros((CHUNK, DIM), F32)
        for head in range(HEADS):
            cols = slice(head * ROWS + part * CHUNK, (head + 1) * ROWS)
            ds = grad_scores(chunk, cols)
            dq = dot(kt[chunk], ds)
            if part == 0:
                dqacc[:, cols] = dq
            else:
                dqacc[:, cols] += dq
            dk = dk + dot(ds, qn[cols, :])
            dv = dv + dot(weights[chunk, :, cols], don[cols, :])
        emit(chunk, dk, dv)

    @pl.loop(first_chunk, REMOTE_CHUNKS)
    def _(chunk):
        for head in range(HEADS):
            cols = slice(head * ROWS, (head + 1) * ROWS)
            ds = grad_scores(chunk, cols)
            dqacc[:, cols] += dot(kt[chunk], ds)
        emit(chunk, dot(ds_ref[...], qn[...]), dot(weights[chunk], don[...]))

    @pl.loop(0, first_chunk)
    def _(chunk):
        emit(chunk, jnp.zeros((CHUNK, DIM), F32), jnp.zeros((CHUNK, DIM), F32))

    for head in range(HEADS):
        dq_ref[head] = dqacc[:, head * ROWS : (head + 1) * ROWS].astype(BF16)


def attend(tp, q, do, own, gathered, swapped):
    vmem = pl.BlockSpec(memory_space=pltpu.VMEM)
    chunks = REMOTE_CHUNKS + 2
    return pl.pallas_call(
        attention_kernel,
        out_shape=(
            jax.ShapeDtypeStruct((HEADS, DIM, ROWS), BF16),
            jax.ShapeDtypeStruct((HEADS, DIM, ROWS), BF16),
            jax.ShapeDtypeStruct((5, 4, PIECE, 2 * DIM), BF16),
        ),
        in_specs=[pl.BlockSpec(memory_space=pltpu.SMEM)] + [vmem] * 8,
        out_specs=(vmem, vmem, vmem),
        scratch_shapes=[
            pltpu.VMEM((chunks, DIM, CHUNK), BF16),
            pltpu.VMEM((chunks, DIM, CHUNK), BF16),
            pltpu.VMEM((chunks, CHUNK, CHUNK), BF16),
            pltpu.VMEM((chunks, CHUNK, DIM), BF16),
            pltpu.VMEM((chunks, CHUNK, COLS), F32),
            pltpu.VMEM((chunks, CHUNK, COLS), BF16),
            pltpu.VMEM((CHUNK, COLS), BF16),
            pltpu.VMEM((CHUNK, COLS), BF16),
            pltpu.VMEM((COLS, DIM), BF16),
            pltpu.VMEM((DIM, COLS), BF16),
            pltpu.VMEM((COLS, DIM), BF16),
            pltpu.VMEM((8, COLS), F32),
            pltpu.VMEM((8, COLS), F32),
            pltpu.VMEM((DIM, COLS), F32),
            pltpu.VMEM((DIM, COLS), F32),
        ],
        compiler_params=pltpu.CompilerParams(vmem_limit_bytes=56 * 1024 * 1024),
        cost_estimate=pl.CostEstimate(flops=8_000_000_000, bytes_accessed=8_000_000, transcendentals=4_000_000),
    )(tp, q, do, own, *gathered, swapped)


def finish_kernel(own_ref, near_ref, far_ref, dk_ref, dv_ref):
    total = own_ref[...].astype(F32) + near_ref[...].astype(F32) + far_ref[...].astype(F32)
    turned = total.T.astype(BF16)
    dk_ref[...] = turned[0:DIM]
    dv_ref[...] = turned[DIM:]


def finish(own, near, far):
    vmem = pl.BlockSpec(memory_space=pltpu.VMEM)
    shape = jax.ShapeDtypeStruct((DIM, PIECE), BF16)
    return pl.pallas_call(
        finish_kernel, out_shape=(shape, shape), in_specs=[vmem] * 3, out_specs=(vmem, vmem)
    )(own, near, far)


def shift(x, by):
    size = lax.axis_size("ctx")
    pairs = [(i, i + by) for i in range(size) if 0 <= i + by < size]
    return lax.ppermute(x, "ctx", pairs)


def swap(x):
    return lax.ppermute(x, "ctx", [(i, i ^ 1) for i in range(lax.axis_size("ctx"))])


def turn(x, by):
    return lax.ppermute(x, "tp", [(i, (i + by) % 4) for i in range(4)])


def local(queries, key_rows, values, grad_out, doc_ids):
    tp = lax.axis_index("tp")
    odd = lax.rem(lax.axis_index("ctx"), 2) == 1
    q = queries.transpose(1, 2, 0)
    do = grad_out.transpose(1, 2, 0)
    docs = jnp.broadcast_to((doc_ids + 1).astype(BF16)[None], (16, ROWS))
    own = jnp.concatenate([key_rows.T, values.T, docs], axis=0)

    def quarter_of(off):
        start = lax.rem(tp + off, 4) * PIECE
        return lax.dynamic_slice(own, (0, start), (PACKED, PIECE))

    mine = quarter_of(0)
    near = shift(mine, 2)
    far = shift(mine, 4)
    pair = jnp.stack([far, near])
    gathered = [pair, turn(pair, 1), turn(pair, -1), turn(pair, 2)]
    payload = jnp.stack(
        [
            jnp.where(odd, piece, jnp.stack([piece[1], quarter_of(off)]))
            for piece, off in zip(gathered, OFFSETS)
        ]
    )
    swapped = swap(payload)
    attended, dq, dkv = attend(tp.astype(jnp.int32)[None], q, do, own, gathered, swapped)
    back = swap(jnp.stack([dkv[1], dkv[3]])).astype(F32)
    a2, a1, a0 = dkv[0].astype(F32), dkv[2].astype(F32), dkv[4].astype(F32)
    a2 = a2 + jnp.where(odd, back[0], 0.0)
    a1 = a1 + jnp.where(odd, back[1], back[0])
    a0 = a0 + jnp.where(odd, 0.0, back[1])
    slots = [jnp.stack([a2[r], a1[r], a0[r]]).astype(BF16) for r in range(4)]
    summed = slots[0].astype(F32)
    for r, by in ((1, -1), (2, 1), (3, 2)):
        summed = summed + turn(slots[r], by).astype(F32)
    summed = summed.astype(BF16)
    dk, dv = finish(summed[2], shift(summed[1], -2), shift(summed[0], -4))
    return attended.transpose(2, 0, 1), dq.transpose(2, 0, 1), dk.T, dv.T


def solution(mesh):
    placed = (P("ctx", "tp", None), P("ctx", None), P("ctx", None), P("ctx", "tp", None), P("ctx"))
    return jax.shard_map(
        local,
        mesh=mesh,
        in_specs=placed,
        out_specs=(
            P("ctx", "tp", None),
            P("ctx", "tp", None),
            P(("ctx", "tp"), None),
            P(("ctx", "tp"), None),
        ),
        check_vma=False,
    )
```

time: 165 us -> 96.3 us (0.58); the launches traced: 164 us -> 97.3 us
  waiting for transfers between devices: 64.7 us -> 36.9 us
  matrix products: 22.5 us -> 0 us
  Pallas kernels: 0 us -> 16.8 us
  between operations: 14.6 us -> 0.89 us
  starting transfers between devices: 46.2 us -> 36.2 us
  other arithmetic: 8.68 us -> 2.81 us
  local copies, waits for them, and re-layouts: 6.94 us -> 3.67 us
    dot_general x18 -> x0, matrix products: 22.5 us -> none  [the longest x3 4.77 us: head_block(): jnp.dot(query_part, key_window.T, preferred_element_type=jnp.float32)]
    unnamed x2 -> x0, waiting for transfers between devices: 19.6 us -> none
    pallas_call x0 -> x2, Pallas kernels: none -> 16.8 us  [the longest x1 15 us: attend(): pl.pallas_call(attention_kernel, out_shape=(jax.ShapeDtypeStruct((HEADS,...]
    ppermute x12, starting transfers between devices: 46.1 us -> 36.2 us  [the longest x4 21.1 us: shift(): return lax.ppermute(x, 'ctx', pairs)]
    ppermute x12, waiting for transfers between devices: 45.2 us -> 36.9 us  [the longest x6 21.1 us: turn(): return lax.ppermute(x, 'tp', [(i, (i + by) % 4) for i in range(4)])]
    unnamed x39 -> x18, local copies, waits for them, and re-layouts: 5.92 us -> 1.56 us
    reduce_sum x3 -> x0, other arithmetic: 2.31 us -> none  [head_block(): probability = exponent / jnp.sum(exponent, axis=-1, keepdims=True)]
    convert_element_type x4 -> x3, other arithmetic: 2.95 us -> 0.94 us  [the longest x1 0.69 us: local(): docs = jnp.broadcast_to((doc_ids + 1).astype(BF16)[None], (16, ROWS))]
  transfers between devices with their start and end apart: 13 -> 12, of which waited for: 8 -> 10; matrix products, arithmetic and copies ran while one was open for 4% -> 0% of each run, Pallas kernels for 0% -> 0%
where the time goes in v1:
time: 96.3 us; the launch traced here: 97.3 us
  waiting for transfers between devices  36.9 us (38%)
  starting transfers between devices  36.2 us (38%)
  Pallas kernels  16.8 us (17%)
  local copies, waits for them, and re-layouts  3.67 us (4%)
  other arithmetic  2.81 us (3%)
    ppermute x4, starting transfers between devices, shift(): return lax.ppermute(x, 'ctx', pairs)  21.1 us
    ppermute x6, waiting for transfers between devices, turn(): return lax.ppermute(x, 'tp', [(i, (i + by) % 4) for i in range(4)])  21.1 us
    pallas_call x1, Pallas kernels, attend(): pl.pallas_call(attention_kernel, out_shape=(jax.ShapeDtypeStruct((HEADS,...  15 us
    ppermute x4, waiting for transfers between devices, shift(): return lax.ppermute(x, 'ctx', pairs)  11.6 us
    ppermute x6, starting transfers between devices, turn(): return lax.ppermute(x, 'tp', [(i, (i + by) % 4) for i in range(4)])  9.92 us
    ppermute x2, starting transfers between devices, swap(): lax.ppermute(x, 'ctx', [(i, i ^ 1) for i in range(lax.axis_size('ctx'))])  5.19 us
    ppermute x2, waiting for transfers between devices, swap(): lax.ppermute(x, 'ctx', [(i, i ^ 1) for i in range(lax.axis_size('ctx'))])  4.23 us
  transfers between devices with their start and end apart: 12, of which 10 were waited for; matrix products, arithmetic and copies ran while one was open for 0% of the time, Pallas kernels for 0%

profile of v1, /device:TPU:102, one launch (start us, length us, event | category | flops | bytes accessed | tf_op | source)
XLA Modules:
  0.0 97.3 jit_solution(7326557685020396831)
XLA Ops:
  0.7 0.7 add_convert_fusion.4
  1.3 1.0 %pad_maximum_fusion.2.own_ref = bf16[400,512]{1,0:T(8,128)(2,1)S(1)} fusion(bf16[16,512]{1,0:T(8,128)(2,1)S(1)} %broadcast_in_dim.16, bf16[192,512]{1,0:T(8,128)(2,1)} %bitcast.61, bf16[192,512]{1,0:T(8,128)(2,1)} %bitcast.62), kind=kLoop, calls=%fused_computation.6 | loop fusion | flops 1228800 | bytes 819200 | tf_op jit(solution)/shard_map/concatenate | solution.py:276
  2.4 0.0 copy-start.1
  2.4 0.1 dynamic-slice_bitcast_fusion.2
  2.5 5.0 %collective-permute-start.1 = (bf16[400,128]{1,0:T(8,128)(2,1)S(1)}, bf16[400,128]{1,0:T(8,128)(2,1)S(1)}, u32[]{:S(2)}, u32[]{:S(2)}) collective-permute-start(bf16[400,128]{1,0:T(8,128)(2,1)S(1)} %get-tuple-element.22), channel_id=1, source_target_pairs={{0,8},{4,12},{8,16},{12,20},{16,24},{20,28},{24,32},{28,36},{32,40... | collective-permute-start | bytes 307208 | tf_op jit(solution)/shard_map/ppermute | solution.py:259
  7.5 4.3 %collective-permute-start = (bf16[400,128]{1,0:T(8,128)(2,1)S(1)}, bf16[400,128]{1,0:T(8,128)(2,1)S(1)}, u32[]{:S(2)}, u32[]{:S(2)}) collective-permute-start(bf16[400,128]{1,0:T(8,128)(2,1)S(1)} %get-tuple-element.22), channel_id=1, source_target_pairs={{0,16},{4,20},{8,24},{12,28},{16,32},{20,36},{24,40},{28,44},{32,4... | collective-permute-start | bytes 307208 | tf_op jit(solution)/shard_map/ppermute | solution.py:259
  11.8 0.0 collective-permute-done.1
  11.8 3.7 %collective-permute-done = bf16[400,128]{1,0:T(8,128)(2,1)S(1)} collective-permute-done((bf16[400,128]{1,0:T(8,128)(2,1)S(1)}, bf16[400,128]{1,0:T(8,128)(2,1)S(1)}, u32[]{:S(2)}, u32[]{:S(2)}) %collective-permute-start) | collective-permute-done | bytes 102432 | tf_op jit(solution)/shard_map/ppermute | solution.py:259
  15.5 0.0 copy-start.5
  15.6 3.3 %collective-permute-start.4 = (bf16[2,400,128]{2,1,0:T(8,128)(2,1)S(1)}, bf16[2,400,128]{2,1,0:T(8,128)(2,1)S(1)}, u32[]{:S(2)}, u32[]{:S(2)}) collective-permute-start(bf16[2,400,128]{2,1,0:T(8,128)(2,1)S(1)} %pad_maximum_fusion.6.g0_ref), channel_id=1, source_target_pairs={{0,2},{1,3},{2,0},{3,1},{4,6},{5,7},{6,4},{7,5},{8,10},{9,11},{10,... | collective-permute-start | bytes 614408 | tf_op jit(solution)/shard_map/ppermute | solution.py:267
  18.8 1.1 %collective-permute-start.3 = (bf16[2,400,128]{2,1,0:T(8,128)(2,1)S(1)}, bf16[2,400,128]{2,1,0:T(8,128)(2,1)S(1)}, u32[]{:S(2)}, u32[]{:S(2)}) collective-permute-start(bf16[2,400,128]{2,1,0:T(8,128)(2,1)S(1)} %pad_maximum_fusion.6.g0_ref), channel_id=1, source_target_pairs={{0,3},{1,0},{2,1},{3,2},{4,7},{5,4},{6,5},{7,6},{8,11},{9,8},{10,9... | collective-permute-start | bytes 614408 | tf_op jit(solution)/shard_map/ppermute | solution.py:267
  19.9 1.0 collective-permute-start.2
  20.9 3.9 %collective-permute-done.4.g3_ref = bf16[2,400,128]{2,1,0:T(8,128)(2,1)S(1)} collective-permute-done((bf16[2,400,128]{2,1,0:T(8,128)(2,1)S(1)}, bf16[2,400,128]{2,1,0:T(8,128)(2,1)S(1)}, u32[]{:S(2)}, u32[]{:S(2)}) %collective-permute-start.4) | collective-permute-done | bytes 204832 | tf_op jit(solution)/shard_map/ppermute | solution.py:267
  24.8 2.4 %collective-permute-done.3.g2_ref = bf16[2,400,128]{2,1,0:T(8,128)(2,1)S(1)} collective-permute-done((bf16[2,400,128]{2,1,0:T(8,128)(2,1)S(1)}, bf16[2,400,128]{2,1,0:T(8,128)(2,1)S(1)}, u32[]{:S(2)}, u32[]{:S(2)}) %collective-permute-start.3) | collective-permute-done | bytes 204832 | tf_op jit(solution)/shard_map/ppermute | solution.py:267
  27.3 0.5 collective-permute-done.2.g1_ref
  27.9 0.0 copy-done.1
  27.9 0.1 pad_maximum_fusion
  28.0 0.0 copy-done.5
  28.0 0.0 copy-done.2
  28.0 0.1 collective-permute-start.5
  28.1 2.3 %collective-permute-done.5.sw_ref = bf16[4,2,400,128]{3,2,1,0:T(8,128)(2,1)S(1)} collective-permute-done((bf16[4,2,400,128]{3,2,1,0:T(8,128)(2,1)S(1)}, bf16[4,2,400,128]{3,2,1,0:T(8,128)(2,1)S(1)}, u32[]{:S(2)}, u32[]{:S(2)}) %collective-permute-start.5) | collective-permute-done | bytes 819232 | tf_op jit(solution)/shard_map/ppermute | solution.py:263
  30.4 0.0 copy-done.3
  30.4 0.0 copy-done.4
  30.4 0.9 copy-done.8
  31.3 15.0 %shard_map.84 = (bf16[3,192,512]{2,1,0:T(8,128)(2,1)}, bf16[3,192,512]{2,1,0:T(8,128)(2,1)}, bf16[5,4,128,384]{3,2,1,0:T(8,128)(2,1)}) custom-call(s32[1]{0:T(128)} %bitcast.tp_ref, bf16[3,192,512]{2,1,0:T(8,128)(2,1)} %bitcast.63, bf16[3,192,512]{2,1,0:T(8,128)(2,1)} %bitcast.64, bf16[400,512]{1,0:T(8,128)(2,1)} %copy-done.1, ...), custom_call_target="tpu_custom_call" | custom-call | flops 8000000000 | bytes 8000000 | tf_op jit(solution)/shard_map/pallas_call | solution.py:210
  46.4 1.2 %fusion.3 = (bf16[1,4,128,384]{3,2,1,0:T(8,128)(2,1)S(1)}, bf16[1,4,128,384]{3,2,1,0:T(8,128)(2,1)S(1)}) fusion(bf16[5,4,128,384]{3,2,1,0:T(8,128)(2,1)} %get-tuple-element.11), kind=kLoop, calls=%fused_computation.38 | loop fusion | bytes 1572864 | tf_op jit(solution)/shard_map/slice | solution.py:295
  47.6 0.0 copy-start
  47.6 0.1 pad_maximum_fusion.1
  47.7 5.1 %collective-permute-start.6 = (bf16[2,4,128,384]{3,2,1,0:T(8,128)(2,1)S(1)}, bf16[2,4,128,384]{3,2,1,0:T(8,128)(2,1)S(1)}, u32[]{:S(2)}, u32[]{:S(2)}) collective-permute-start(bf16[2,4,128,384]{3,2,1,0:T(8,128)(2,1)S(1)} %pad_maximum_fusion.1), channel_id=1, source_target_pairs={{0,4},{4,0},{8,12},{12,8},{16,20},{20,16},{24,28},{28,24},{32,36},... | collective-permute-start | bytes 2359304 | tf_op jit(solution)/shard_map/ppermute | solution.py:263
  52.8 1.9 %collective-permute-done.6 = bf16[2,4,128,384]{3,2,1,0:T(8,128)(2,1)S(1)} collective-permute-done((bf16[2,4,128,384]{3,2,1,0:T(8,128)(2,1)S(1)}, bf16[2,4,128,384]{3,2,1,0:T(8,128)(2,1)S(1)}, u32[]{:S(2)}, u32[]{:S(2)}) %collective-permute-start.6) | collective-permute-done | bytes 786464 | tf_op jit(solution)/shard_map/ppermute | solution.py:263
  54.7 0.1 convert_element_type.39
  54.8 0.0 copy-done
  54.8 0.3 add_convert_fusion.2
  55.2 0.1 slice_bitcast_fusion.12
  55.3 2.3 %collective-permute-start.7 = (bf16[3,128,384]{2,1,0:T(8,128)(2,1)S(1)}, bf16[3,128,384]{2,1,0:T(8,128)(2,1)S(1)}, u32[]{:S(2)}, u32[]{:S(2)}) collective-permute-start(bf16[3,128,384]{2,1,0:T(8,128)(2,1)S(1)} %pad_maximum_fusion.3), channel_id=1, source_target_pairs={{0,3},{1,0},{2,1},{3,2},{4,7},{5,4},{6,5},{7,6},{8,11},{9,8},{10,9... | collective-permute-start | bytes 884744 | tf_op jit(solution)/shard_map/ppermute | solution.py:267
  57.7 0.1 collective-permute-start.8
  57.9 2.2 %collective-permute-start.9 = (bf16[3,128,384]{2,1,0:T(8,128)(2,1)S(1)}, bf16[3,128,384]{2,1,0:T(8,128)(2,1)S(1)}, u32[]{:S(2)}, u32[]{:S(2)}) collective-permute-start(bf16[3,128,384]{2,1,0:T(8,128)(2,1)S(1)} %pad_maximum_fusion.5), channel_id=1, source_target_pairs={{0,2},{1,3},{2,0},{3,1},{4,6},{5,7},{6,4},{7,5},{8,10},{9,11},{10,... | collective-permute-start | bytes 884744 | tf_op jit(solution)/shard_map/ppermute | solution.py:267
  60.1 10.7 %collective-permute-done.7 = bf16[3,128,384]{2,1,0:T(8,128)(2,1)S(1)} collective-permute-done((bf16[3,128,384]{2,1,0:T(8,128)(2,1)S(1)}, bf16[3,128,384]{2,1,0:T(8,128)(2,1)S(1)}, u32[]{:S(2)}, u32[]{:S(2)}) %collective-permute-start.7) | collective-permute-done | bytes 294944 | tf_op jit(solution)/shard_map/ppermute | solution.py:267
  70.8 3.5 %collective-permute-done.8 = bf16[3,128,384]{2,1,0:T(8,128)(2,1)S(1)} collective-permute-done((bf16[3,128,384]{2,1,0:T(8,128)(2,1)S(1)}, bf16[3,128,384]{2,1,0:T(8,128)(2,1)S(1)}, u32[]{:S(2)}, u32[]{:S(2)}) %collective-permute-start.8) | collective-permute-done | bytes 294944 | tf_op jit(solution)/shard_map/ppermute | solution.py:267
  74.3 0.0 collective-permute-done.9
  74.3 0.2 add_convert_fusion.3
  74.5 0.7 slice_bitcast_fusion
  75.2 9.9 %collective-permute-start.11 = (bf16[128,384]{1,0:T(8,128)(2,1)S(1)}, bf16[128,384]{1,0:T(8,128)(2,1)S(1)}, u32[]{:S(2)}, u32[]{:S(2)}) collective-permute-start(bf16[128,384]{1,0:T(8,128)(2,1)S(1)} %get-tuple-element.35), channel_id=1, source_target_pairs={{16,0},{20,4},{24,8},{28,12},{32,16},{36,20},{40,24},{44,28},{48,3... | collective-permute-start | bytes 294920 | tf_op jit(solution)/shard_map/ppermute | solution.py:259
  85.1 1.9 %collective-permute-start.10 = (bf16[128,384]{1,0:T(8,128)(2,1)S(1)}, bf16[128,384]{1,0:T(8,128)(2,1)S(1)}, u32[]{:S(2)}, u32[]{:S(2)}) collective-permute-start(bf16[128,384]{1,0:T(8,128)(2,1)S(1)} %get-tuple-element.36), channel_id=1, source_target_pairs={{8,0},{12,4},{16,8},{20,12},{24,16},{28,20},{32,24},{36,28},{40,32... | collective-permute-start | bytes 294920 | tf_op jit(solution)/shard_map/ppermute | solution.py:259
  87.0 0.3 collective-permute-done.11.far_ref
  87.3 7.6 %collective-permute-done.10.near_ref = bf16[128,384]{1,0:T(8,128)(2,1)S(1)} collective-permute-done((bf16[128,384]{1,0:T(8,128)(2,1)S(1)}, bf16[128,384]{1,0:T(8,128)(2,1)S(1)}, u32[]{:S(2)}, u32[]{:S(2)}) %collective-permute-start.10) | collective-permute-done | bytes 98336 | tf_op jit(solution)/shard_map/ppermute | solution.py:259
  94.9 0.6 copy-done.7
  95.5 1.7 %shard_map.85 = (bf16[192,128]{1,0:T(8,128)(2,1)}, bf16[192,128]{1,0:T(8,128)(2,1)}) custom-call(bf16[128,384]{1,0:T(8,128)(2,1)} %get-tuple-element.37.own_ref, bf16[128,384]{1,0:T(8,128)(2,1)} %copy-done.7, bf16[128,384]{1,0:T(8,128)(2,1)} %copy-done.6), custom_call_target="tpu_custom_call" | custom-call | tf_op jit(solution)/shard_map/pallas_call | solution.py:251
  (20 shorter events, 0.4 us)
Async XLA Ops:
  2.4 25.5 %copy-start.1 = (bf16[400,512]{1,0:T(8,128)(2,1)}, bf16[400,512]{1,0:T(8,128)(2,1)S(1)}, u32[]{:S(2)}) copy-start(bf16[400,512]{1,0:T(8,128)(2,1)S(1)} %pad_maximum_fusion.2.own_ref) | copy-start | bytes 1228804
  2.5 9.3 %collective-permute-start.1 = (bf16[400,128]{1,0:T(8,128)(2,1)S(1)}, bf16[400,128]{1,0:T(8,128)(2,1)S(1)}, u32[]{:S(2)}, u32[]{:S(2)}) collective-permute-start(bf16[400,128]{1,0:T(8,128)(2,1)S(1)} %get-tuple-element.22), channel_id=1, source_target_pairs={{0,8},{4,12},{8,16},{12,20},{16,24},{20,28},{24,32},{28,36},{32,40... | collective-permute-start | bytes 307208 | tf_op jit(solution)/shard_map/ppermute | solution.py:259
  7.5 8.1 %collective-permute-start = (bf16[400,128]{1,0:T(8,128)(2,1)S(1)}, bf16[400,128]{1,0:T(8,128)(2,1)S(1)}, u32[]{:S(2)}, u32[]{:S(2)}) collective-permute-start(bf16[400,128]{1,0:T(8,128)(2,1)S(1)} %get-tuple-element.22), channel_id=1, source_target_pairs={{0,16},{4,20},{8,24},{12,28},{16,32},{20,36},{24,40},{28,44},{32,4... | collective-permute-start | bytes 307208 | tf_op jit(solution)/shard_map/ppermute | solution.py:259
  15.5 12.4 %copy-start.5 = (bf16[2,400,128]{2,1,0:T(8,128)(2,1)}, bf16[2,400,128]{2,1,0:T(8,128)(2,1)S(1)}, u32[]{:S(2)}) copy-start(bf16[2,400,128]{2,1,0:T(8,128)(2,1)S(1)} %pad_maximum_fusion.6.g0_ref) | copy-start | bytes 614404
  15.6 9.3 %collective-permute-start.4 = (bf16[2,400,128]{2,1,0:T(8,128)(2,1)S(1)}, bf16[2,400,128]{2,1,0:T(8,128)(2,1)S(1)}, u32[]{:S(2)}, u32[]{:S(2)}) collective-permute-start(bf16[2,400,128]{2,1,0:T(8,128)(2,1)S(1)} %pad_maximum_fusion.6.g0_ref), channel_id=1, source_target_pairs={{0,2},{1,3},{2,0},{3,1},{4,6},{5,7},{6,4},{7,5},{8,10},{9,11},{10,... | collective-permute-start | bytes 614408 | tf_op jit(solution)/shard_map/ppermute | solution.py:267
  18.8 8.4 %collective-permute-start.3 = (bf16[2,400,128]{2,1,0:T(8,128)(2,1)S(1)}, bf16[2,400,128]{2,1,0:T(8,128)(2,1)S(1)}, u32[]{:S(2)}, u32[]{:S(2)}) collective-permute-start(bf16[2,400,128]{2,1,0:T(8,128)(2,1)S(1)} %pad_maximum_fusion.6.g0_ref), channel_id=1, source_target_pairs={{0,3},{1,0},{2,1},{3,2},{4,7},{5,4},{6,5},{7,6},{8,11},{9,8},{10,9... | collective-permute-start | bytes 614408 | tf_op jit(solution)/shard_map/ppermute | solution.py:267
  19.9 7.8 %collective-permute-start.2 = (bf16[2,400,128]{2,1,0:T(8,128)(2,1)S(1)}, bf16[2,400,128]{2,1,0:T(8,128)(2,1)S(1)}, u32[]{:S(2)}, u32[]{:S(2)}) collective-permute-start(bf16[2,400,128]{2,1,0:T(8,128)(2,1)S(1)} %pad_maximum_fusion.6.g0_ref), channel_id=1, source_target_pairs={{0,1},{1,2},{2,3},{3,0},{4,5},{5,6},{6,7},{7,4},{8,9},{9,10},{10,1... | collective-permute-start | bytes 614408 | tf_op jit(solution)/shard_map/ppermute | solution.py:267
  24.8 3.2 %copy-start.2 = (bf16[2,400,128]{2,1,0:T(8,128)(2,1)}, bf16[2,400,128]{2,1,0:T(8,128)(2,1)S(1)}, u32[]{:S(2)}) copy-start(bf16[2,400,128]{2,1,0:T(8,128)(2,1)S(1)} %collective-permute-done.4.g3_ref) | copy-start | bytes 614404
  27.3 3.2 %copy-start.3 = (bf16[2,400,128]{2,1,0:T(8,128)(2,1)}, bf16[2,400,128]{2,1,0:T(8,128)(2,1)S(1)}, u32[]{:S(2)}) copy-start(bf16[2,400,128]{2,1,0:T(8,128)(2,1)S(1)} %collective-permute-done.3.g2_ref) | copy-start | bytes 614404
  27.7 2.7 %copy-start.4 = (bf16[2,400,128]{2,1,0:T(8,128)(2,1)}, bf16[2,400,128]{2,1,0:T(8,128)(2,1)S(1)}, u32[]{:S(2)}) copy-start(bf16[2,400,128]{2,1,0:T(8,128)(2,1)S(1)} %collective-permute-done.2.g1_ref) | copy-start | bytes 614404
  28.0 2.4 %collective-permute-start.5 = (bf16[4,2,400,128]{3,2,1,0:T(8,128)(2,1)S(1)}, bf16[4,2,400,128]{3,2,1,0:T(8,128)(2,1)S(1)}, u32[]{:S(2)}, u32[]{:S(2)}) collective-permute-start(bf16[4,2,400,128]{3,2,1,0:T(8,128)(2,1)S(1)} %pad_maximum_fusion), channel_id=1, source_target_pairs={{0,4},{4,0},{8,12},{12,8},{16,20},{20,16},{24,28},{28,24},{32,36},... | collective-permute-start | bytes 2457608 | tf_op jit(solution)/shard_map/ppermute | solution.py:263
  30.4 0.9 copy-start.8
  47.6 7.2 %copy-start = (bf16[5,4,128,384]{3,2,1,0:T(8,128)(2,1)S(1)}, bf16[5,4,128,384]{3,2,1,0:T(8,128)(2,1)}, u32[]{:S(2)}) copy-start(bf16[5,4,128,384]{3,2,1,0:T(8,128)(2,1)} %get-tuple-element.11) | copy-start | bytes 5898244
  47.7 7.0 %collective-permute-start.6 = (bf16[2,4,128,384]{3,2,1,0:T(8,128)(2,1)S(1)}, bf16[2,4,128,384]{3,2,1,0:T(8,128)(2,1)S(1)}, u32[]{:S(2)}, u32[]{:S(2)}) collective-permute-start(bf16[2,4,128,384]{3,2,1,0:T(8,128)(2,1)S(1)} %pad_maximum_fusion.1), channel_id=1, source_target_pairs={{0,4},{4,0},{8,12},{12,8},{16,20},{20,16},{24,28},{28,24},{32,36},... | collective-permute-start | bytes 2359304 | tf_op jit(solution)/shard_map/ppermute | solution.py:263
  55.3 15.5 %collective-permute-start.7 = (bf16[3,128,384]{2,1,0:T(8,128)(2,1)S(1)}, bf16[3,128,384]{2,1,0:T(8,128)(2,1)S(1)}, u32[]{:S(2)}, u32[]{:S(2)}) collective-permute-start(bf16[3,128,384]{2,1,0:T(8,128)(2,1)S(1)} %pad_maximum_fusion.3), channel_id=1, source_target_pairs={{0,3},{1,0},{2,1},{3,2},{4,7},{5,4},{6,5},{7,6},{8,11},{9,8},{10,9... | collective-permute-start | bytes 884744 | tf_op jit(solution)/shard_map/ppermute | solution.py:267
  57.7 16.6 %collective-permute-start.8 = (bf16[3,128,384]{2,1,0:T(8,128)(2,1)S(1)}, bf16[3,128,384]{2,1,0:T(8,128)(2,1)S(1)}, u32[]{:S(2)}, u32[]{:S(2)}) collective-permute-start(bf16[3,128,384]{2,1,0:T(8,128)(2,1)S(1)} %pad_maximum_fusion.4), channel_id=1, source_target_pairs={{0,1},{1,2},{2,3},{3,0},{4,5},{5,6},{6,7},{7,4},{8,9},{9,10},{10,1... | collective-permute-start | bytes 884744 | tf_op jit(solution)/shard_map/ppermute | solution.py:267
  57.9 16.5 %collective-permute-start.9 = (bf16[3,128,384]{2,1,0:T(8,128)(2,1)S(1)}, bf16[3,128,384]{2,1,0:T(8,128)(2,1)S(1)}, u32[]{:S(2)}, u32[]{:S(2)}) collective-permute-start(bf16[3,128,384]{2,1,0:T(8,128)(2,1)S(1)} %pad_maximum_fusion.5), channel_id=1, source_target_pairs={{0,2},{1,3},{2,0},{3,1},{4,6},{5,7},{6,4},{7,5},{8,10},{9,11},{10,... | collective-permute-start | bytes 884744 | tf_op jit(solution)/shard_map/ppermute | solution.py:267
  75.2 12.1 %collective-permute-start.11 = (bf16[128,384]{1,0:T(8,128)(2,1)S(1)}, bf16[128,384]{1,0:T(8,128)(2,1)S(1)}, u32[]{:S(2)}, u32[]{:S(2)}) collective-permute-start(bf16[128,384]{1,0:T(8,128)(2,1)S(1)} %get-tuple-element.35), channel_id=1, source_target_pairs={{16,0},{20,4},{24,8},{28,12},{32,16},{36,20},{40,24},{44,28},{48,3... | collective-permute-start | bytes 294920 | tf_op jit(solution)/shard_map/ppermute | solution.py:259
  85.1 9.8 %collective-permute-start.10 = (bf16[128,384]{1,0:T(8,128)(2,1)S(1)}, bf16[128,384]{1,0:T(8,128)(2,1)S(1)}, u32[]{:S(2)}, u32[]{:S(2)}) collective-permute-start(bf16[128,384]{1,0:T(8,128)(2,1)S(1)} %get-tuple-element.36), channel_id=1, source_target_pairs={{8,0},{12,4},{16,8},{20,12},{24,16},{28,20},{32,24},{36,28},{40,32... | collective-permute-start | bytes 294920 | tf_op jit(solution)/shard_map/ppermute | solution.py:259
  87.3 7.6 %copy-start.6 = (bf16[128,384]{1,0:T(8,128)(2,1)}, bf16[128,384]{1,0:T(8,128)(2,1)S(1)}, u32[]{:S(2)}) copy-start(bf16[128,384]{1,0:T(8,128)(2,1)S(1)} %collective-permute-done.11.far_ref) | copy-start | bytes 294916
  94.9 0.6 copy-start.7

commit v2 on v0

v2 whole, which is shorter than its diff:
```python
import jax
import jax.numpy as jnp
from jax import lax
from jax.experimental import pallas as pl
from jax.experimental.pallas import tpu as pltpu
from jax.sharding import PartitionSpec as P

LOG2E = 1.4426950408889634
NEGATIVE = -1e30
ROWS = 512
HALF = 256
PIECE = 128
DIM = 192
WIDE = 256
DOC_ROW = 2 * DIM
PACKED = DOC_ROW + 16
TILES = 4
HEADS = 3
COLS = HEADS * ROWS
SCALE = DIM ** -0.5
OFFSETS = (0, 3, 1, 2)
F32 = jnp.float32
BF16 = jnp.bfloat16
VMEM = pl.BlockSpec(memory_space=pltpu.VMEM)
SMEM = pl.BlockSpec(memory_space=pltpu.SMEM)


def dot(a, b):
    return jnp.dot(a, b, preferred_element_type=F32)


def head_cols(head, start=0):
    return slice(head * ROWS + start, (head + 1) * ROWS)


def one_hot(docs, width):
    rows = lax.broadcasted_iota(jnp.int32, (64, width), 0).astype(F32)
    return rows == docs.astype(F32)


def key_features(piece):
    hot = one_hot(piece[DOC_ROW : DOC_ROW + 1, :], piece.shape[1])
    return jnp.concatenate([piece[0:DIM, :], hot.astype(F32).astype(BF16)], axis=0).T


def folded(x):
    return x.reshape(x.shape[0] // 8, 8, x.shape[1])


def spread(row):
    return jnp.broadcast_to(row, (8, row.shape[1]))


def relative_slot(quarter, tp):
    off = lax.rem(quarter - tp + 4, 4)
    return jnp.where(off == 0, 0, jnp.where(off == 3, 1, off + 1))


def own_kernel(q_ref, own_ref, qe, qn, w_ref, top_ref, total_ref, o_ref):
    docs = own_ref[DOC_ROW : DOC_ROW + 1, :]
    mask_rows = jnp.where(one_hot(docs, ROWS), 0.0, NEGATIVE).astype(BF16)
    kn = key_features(own_ref[...])
    causal = lax.broadcasted_iota(jnp.int32, (HALF, HALF), 0) <= lax.broadcasted_iota(
        jnp.int32, (HALF, HALF), 1
    )
    for head in range(HEADS):
        cols = head_cols(head)
        low = slice(head * ROWS, head * ROWS + HALF)
        high = head_cols(head, HALF)
        qe[0:DIM, cols] = q_ref[head]
        qe[DIM:, cols] = mask_rows
        qn[cols, :] = q_ref[head].T
        s_low = jnp.where(causal, dot(kn[0:HALF], qe[:, low]), NEGATIVE)
        s_high = dot(kn, qe[:, high])
        s_top = s_high[0:HALF]
        s_last = jnp.where(causal, s_high[HALF:], NEGATIVE)
        for span, parts in ((low, (s_low,)), (high, (s_top, s_last))):
            peak = jnp.max(folded(parts[0]), axis=0)
            for s in parts[1:]:
                peak = jnp.maximum(peak, jnp.max(folded(s), axis=0))
            peak = spread(jnp.max(peak, axis=0, keepdims=True) * (SCALE * LOG2E))
            top_ref[:, span] = peak
            total = jnp.zeros((8, HALF), F32)
            for part, s in enumerate(parts):
                e = jnp.exp2(folded(s) * (SCALE * LOG2E) - peak[None])
                total = total + jnp.sum(e, axis=0)
                w_ref[part * HALF : (part + 1) * HALF, span] = e.reshape(HALF, HALF).astype(BF16)
            total_ref[:, span] = total
        o_ref[:, low] = dot(own_ref[DIM : 2 * DIM, 0:HALF], w_ref[0:HALF, low])
        o_ref[:, high] = dot(own_ref[DIM : 2 * DIM, :], w_ref[:, high])


def own_forward(q, own):
    return pl.pallas_call(
        own_kernel,
        out_shape=(
            jax.ShapeDtypeStruct((WIDE, COLS), BF16),
            jax.ShapeDtypeStruct((COLS, DIM), BF16),
            jax.ShapeDtypeStruct((ROWS, COLS), BF16),
            jax.ShapeDtypeStruct((8, COLS), F32),
            jax.ShapeDtypeStruct((8, COLS), F32),
            jax.ShapeDtypeStruct((DIM, COLS), F32),
        ),
        in_specs=[VMEM] * 2,
        out_specs=(VMEM,) * 6,
        compiler_params=pltpu.CompilerParams(vmem_limit_bytes=8 * 1024 * 1024),
        cost_estimate=pl.CostEstimate(flops=800_000_000, bytes_accessed=8_000_000, transcendentals=600_000),
    )(q, own)


def earlier_kernel(
    tp_ref, do_ref, docs_ref, qe, qn, top0_ref, total0_ref, o0_ref,
    a2_refs, a1_refs, sw_ref,
    o_ref, dkv_ref, ds_ref, kt, stats_ref, first_ref,
    vt, kn, vn, scores, weights, dop, don, top, total, oacc,
):
    tp = tp_ref[0]
    to_log2 = SCALE * LOG2E

    def piece_of(tile, slot):
        if tile % 2 == 0:
            return (a2_refs, a1_refs)[tile // 2][slot]
        return sw_ref.at[slot, tile // 2]

    first_doc = docs_ref[0:1, 0:1].astype(F32)
    matches = jnp.zeros((1, PIECE), F32)
    for tile in range(TILES):
        for slot in range(4):
            docs = piece_of(tile, slot)[DOC_ROW : DOC_ROW + 1, :].astype(F32)
            matches = matches + jnp.where(docs == first_doc, 1.0, 0.0)
    reach = jnp.sum(matches).astype(jnp.int32)
    first = (TILES * ROWS - reach) // ROWS
    first_ref[0] = first

    for tile in range(TILES):
        @pl.when(tile >= first)
        def _():
            for slot in range(4):
                start = lax.rem(tp + OFFSETS[slot], 4) * PIECE
                span = pl.ds(pl.multiple_of(start, PIECE), PIECE)
                piece = piece_of(tile, slot)[...]
                kt[tile, :, span] = piece[0:DIM, :]
                vt[tile, :, span] = piece[DIM : 2 * DIM, :]
                kn[tile, span, :] = key_features(piece)
                vn[tile, span, :] = piece[DIM : 2 * DIM, :].T

    top[...] = top0_ref[...] * (1.0 / to_log2)

    @pl.loop(first, TILES)
    def _(tile):
        for head in range(HEADS):
            cols = head_cols(head)
            s = dot(kn[tile], qe[:, cols])
            scores[tile, :, cols] = s
            top[:, cols] = jnp.maximum(top[:, cols], jnp.max(folded(s), axis=0))

    top[...] = spread(jnp.max(top[...], axis=0, keepdims=True) * to_log2)
    shrink = jnp.exp2(top0_ref[...] - top[...])
    total[...] = total0_ref[...] * shrink
    for head in range(HEADS):
        cols = head_cols(head)
        oacc[:, cols] = o0_ref[:, cols] * shrink[0:1, cols]

    @pl.loop(first, TILES)
    def _(tile):
        for head in range(HEADS):
            cols = head_cols(head)
            e = jnp.exp2(folded(scores[tile, :, cols]) * to_log2 - top[:, cols][None])
            total[:, cols] += jnp.sum(e, axis=0)
            w = e.reshape(ROWS, ROWS).astype(BF16)
            weights[tile, :, cols] = w
            oacc[:, cols] += dot(vt[tile], w)

    for head in range(HEADS):
        cols = head_cols(head)
        inverse = 1.0 / jnp.sum(total[:, cols], axis=0, keepdims=True)
        attended = (oacc[:, cols] * inverse).astype(BF16)
        o_ref[head] = attended
        grads = do_ref[head].astype(F32)
        delta = jnp.sum(grads * attended.astype(F32), axis=0, keepdims=True)
        ratio = inverse * SCALE
        top[:, cols] = spread(delta * ratio)
        stats_ref[0:8, cols] = spread(ratio * shrink[0:1, cols])
        stats_ref[8:16, cols] = spread(delta * ratio * shrink[0:1, cols])
        scaled = (grads * ratio).astype(BF16)
        dop[:, cols] = scaled
        don[cols, :] = scaled.T

    @pl.loop(first, TILES)
    def _(tile):
        for head in range(HEADS):
            cols = head_cols(head)
            dp = folded(dot(vn[tile], dop[:, cols]))
            w = folded(weights[tile, :, cols].astype(F32))
            ds_ref[tile, :, cols] = (w * (dp - top[:, cols][None])).reshape(ROWS, ROWS).astype(BF16)
        dk = dot(ds_ref[tile], qn[...])
        dv = dot(weights[tile], don[...])
        both = jnp.concatenate([dk, dv * (1.0 / SCALE)], axis=1).astype(BF16)
        for quarter in range(4):
            dkv_ref[tile, relative_slot(quarter, tp)] = both[quarter * PIECE : (quarter + 1) * PIECE]

    @pl.loop(0, first)
    def _(tile):
        dkv_ref[tile] = jnp.zeros((4, PIECE, 2 * DIM), BF16)


def earlier(tp, do, docs, own_parts, far, near, swapped):
    qe, qn, _, top, total, o = own_parts
    def kernel(*refs):
        earlier_kernel(*refs[:8], refs[8:12], refs[12:16], *refs[16:])
    return pl.pallas_call(
        kernel,
        out_shape=(
            jax.ShapeDtypeStruct((HEADS, DIM, ROWS), BF16),
            jax.ShapeDtypeStruct((TILES, 4, PIECE, 2 * DIM), BF16),
            jax.ShapeDtypeStruct((TILES, ROWS, COLS), BF16),
            jax.ShapeDtypeStruct((TILES, DIM, ROWS), BF16),
            jax.ShapeDtypeStruct((16, COLS), F32),
            jax.ShapeDtypeStruct((1,), jnp.int32),
        ),
        in_specs=[SMEM] + [VMEM] * 16,
        out_specs=(VMEM,) * 5 + (SMEM,),
        scratch_shapes=[
            pltpu.VMEM((TILES, DIM, ROWS), BF16),
            pltpu.VMEM((TILES, ROWS, WIDE), BF16),
            pltpu.VMEM((TILES, ROWS, DIM), BF16),
            pltpu.VMEM((TILES, ROWS, COLS), F32),
            pltpu.VMEM((TILES, ROWS, COLS), BF16),
            pltpu.VMEM((DIM, COLS), BF16),
            pltpu.VMEM((COLS, DIM), BF16),
            pltpu.VMEM((8, COLS), F32),
            pltpu.VMEM((8, COLS), F32),
            pltpu.VMEM((DIM, COLS), F32),
        ],
        compiler_params=pltpu.CompilerParams(vmem_limit_bytes=30 * 1024 * 1024),
        cost_estimate=pl.CostEstimate(flops=8_000_000_000, bytes_accessed=8_000_000, transcendentals=4_000_000),
    )(tp, do, docs, qe, qn, top, total, o, *far, *near, swapped)


def own_back_kernel(
    tp_ref, first_ref, do_ref, own_ref, qn, w_ref, stats_ref, ds_ref, kt,
    dq_ref, dkv_ref, ds_own, don, dqacc,
):
    tp = tp_ref[0]
    vn = own_ref[DIM : 2 * DIM, :].T
    for head in range(HEADS):
        cols = head_cols(head)
        low = slice(head * ROWS, head * ROWS + HALF)
        high = head_cols(head, HALF)
        scaled = (do_ref[head].astype(F32) * stats_ref[0:1, cols]).astype(BF16)
        don[cols, :] = scaled.T
        dp_low = dot(vn[0:HALF], scaled[:, 0:HALF])
        dp_high = dot(vn, scaled[:, HALF:])
        ds_own[0:HALF, low] = (
            w_ref[0:HALF, low].astype(F32) * (dp_low - stats_ref[8:9, low])
        ).astype(BF16)
        ds_own[:, high] = (w_ref[:, high].astype(F32) * (dp_high - stats_ref[8:9, high])).astype(BF16)
        dqacc[:, low] = dot(own_ref[0:DIM, 0:HALF], ds_own[0:HALF, low])
        dqacc[:, high] = dot(own_ref[0:DIM, :], ds_own[:, high])
    for part in range(2):
        span = slice(part * HALF, (part + 1) * HALF)
        dk = jnp.zeros((HALF, DIM), F32)
        dv = jnp.zeros((HALF, DIM), F32)
        for head in range(HEADS):
            cols = head_cols(head, part * HALF)
            dk = dk + dot(ds_own[span, cols], qn[cols, :])
            dv = dv + dot(w_ref[span, cols], don[cols, :])
        both = jnp.concatenate([dk, dv * (1.0 / SCALE)], axis=1).astype(BF16)
        for half in range(2):
            slot = relative_slot(part * 2 + half, tp)
            dkv_ref[slot] = both[half * PIECE : (half + 1) * PIECE]

    @pl.loop(first_ref[0], TILES)
    def _(tile):
        for head in range(HEADS):
            cols = head_cols(head)
            dqacc[:, cols] += dot(kt[tile], ds_ref[tile, :, cols])

    for head in range(HEADS):
        dq_ref[head] = dqacc[:, head_cols(head)].astype(BF16)


def own_back(tp, first, do, own, own_parts, stats, ds, kt):
    return pl.pallas_call(
        own_back_kernel,
        out_shape=(
            jax.ShapeDtypeStruct((HEADS, DIM, ROWS), BF16),
            jax.ShapeDtypeStruct((4, PIECE, 2 * DIM), BF16),
        ),
        in_specs=[SMEM, SMEM] + [VMEM] * 7,
        out_specs=(VMEM,) * 2,
        scratch_shapes=[
            pltpu.VMEM((ROWS, COLS), BF16),
            pltpu.VMEM((COLS, DIM), BF16),
            pltpu.VMEM((DIM, COLS), F32),
        ],
        compiler_params=pltpu.CompilerParams(vmem_limit_bytes=8 * 1024 * 1024),
        cost_estimate=pl.CostEstimate(flops=2_000_000_000, bytes_accessed=8_000_000, transcendentals=0),
    )(tp, first, do, own, own_parts[1], own_parts[2], stats, ds, kt)


def finish_kernel(*refs):
    total = refs[0][...].astype(F32)
    for ref in refs[1:-2]:
        total = total + ref[...].astype(F32)
    turned = total.T.astype(BF16)
    refs[-2][...] = turned[0:DIM]
    refs[-1][...] = turned[DIM:]


def finish(parts):
    shape = jax.ShapeDtypeStruct((DIM, PIECE), BF16)
    return pl.pallas_call(
        finish_kernel, out_shape=(shape, shape), in_specs=[VMEM] * len(parts), out_specs=(VMEM, VMEM)
    )(*parts)


def shift(x, by):
    size = lax.axis_size("ctx")
    pairs = [(i, i + by) for i in range(size) if 0 <= i + by < size]
    return lax.ppermute(x, "ctx", pairs)


def swap(x):
    return lax.ppermute(x, "ctx", [(i, i ^ 1) for i in range(lax.axis_size("ctx"))])


def turn(x, by):
    return lax.ppermute(x, "tp", [(i, (i + by) % 4) for i in range(4)])


def local(queries, key_rows, values, grad_out, doc_ids):
    tp = lax.axis_index("tp")
    tp_scalar = tp.astype(jnp.int32)[None]
    odd = lax.rem(lax.axis_index("ctx"), 2) == 1
    q = queries.transpose(1, 2, 0)
    do = grad_out.transpose(1, 2, 0)
    docs = jnp.broadcast_to((doc_ids + 1).astype(BF16)[None], (16, ROWS))
    own = jnp.concatenate([key_rows.T, values.T, docs], axis=0)

    def quarter_of(x, off):
        start = lax.rem(tp + off, 4) * PIECE
        return lax.dynamic_slice(x, (0, start), (PACKED, PIECE))

    far = shift(quarter_of(own, 0), 4)
    near_whole = shift(own, 2)
    own_parts = own_forward(q, own)
    far, own_parts = lax.optimization_barrier((far, own_parts))
    fars = [far, turn(far, 1), turn(far, -1), turn(far, 2)]
    nears = [quarter_of(near_whole, off) for off in OFFSETS]
    owns = [quarter_of(own, off) for off in OFFSETS]
    payload = jnp.stack(
        [jnp.stack([jnp.where(odd, f, n), jnp.where(odd, n, o)]) for f, n, o in zip(fars, nears, owns)]
    )
    swapped = swap(payload)
    attended, dkv, ds, kt, stats, first = earlier(tp_scalar, do, docs, own_parts, fars, nears, swapped)
    back = swap(jnp.stack([dkv[1], dkv[3]]))
    a2 = [dkv[0, r].astype(F32) + jnp.where(odd, back[0, r].astype(F32), 0.0) for r in range(4)]
    a1 = dkv[2].astype(F32) + jnp.where(odd, back[1], back[0]).astype(F32)
    a1_here = shift(a1.astype(BF16), -2)
    a2_sum = a2[0]
    for r, by in ((1, -1), (2, 1), (3, 2)):
        a2_sum = a2_sum + turn(a2[r].astype(BF16), by).astype(F32)
    a2_here = shift(a2_sum.astype(BF16), -4)
    dq, dkv_own = own_back(tp_scalar, first, do, own, own_parts, stats, ds, kt)
    a0 = [
        dkv_own[r].astype(F32) + a1_here[r].astype(F32) + jnp.where(odd, 0.0, back[1, r].astype(F32))
        for r in range(4)
    ]
    parts = [a0[0], a2_here]
    for r, by in ((1, -1), (2, 1), (3, 2)):
        parts.append(turn(a0[r].astype(BF16), by))
    dk, dv = finish(parts)
    return attended.transpose(2, 0, 1), dq.transpose(2, 0, 1), dk.T, dv.T


def solution(mesh):
    placed = (P("ctx", "tp", None), P("ctx", None), P("ctx", None), P("ctx", "tp", None), P("ctx"))
    return jax.shard_map(
        local,
        mesh=mesh,
        in_specs=placed,
        out_specs=(
            P("ctx", "tp", None),
            P("ctx", "tp", None),
            P(("ctx", "tp"), None),
            P(("ctx", "tp"), None),
        ),
        check_vma=False,
    )
```

time: 165 us -> 82 us (0.50)
  waiting for transfers between devices: 64.7 us -> 27.2 us
  matrix products: 22.5 us -> 0 us
  starting transfers between devices: 46.2 us -> 30 us
  Pallas kernels: 0 us -> 15.4 us
  between operations: 14.6 us -> 0.84 us
  other arithmetic: 8.68 us -> 4.52 us
  local copies, waits for them, and re-layouts: 6.94 us -> 3.72 us
    dot_general x18 -> x0, matrix products: 22.5 us -> none  [the longest x3 4.77 us: head_block(): jnp.dot(query_part, key_window.T, preferred_element_type=jnp.float32)]
    unnamed x2 -> x0, waiting for transfers between devices: 19.6 us -> none
    ppermute x12 -> x15, waiting for transfers between devices: 45.2 us -> 27.2 us  [the longest x4 14.2 us: shift(): return lax.ppermute(x, 'ctx', pairs)]
    ppermute x12 -> x15, starting transfers between devices: 46.1 us -> 30 us  [the longest x4 15.2 us: shift(): return lax.ppermute(x, 'ctx', pairs)]
    pallas_call x0 -> x4, Pallas kernels: none -> 15.4 us  [the longest x1 7.93 us: earlier(): pl.pallas_call(kernel, out_shape=(jax.ShapeDtypeStruct((HEADS, DIM, ROWS)...]
    unnamed x39 -> x20, local copies, waits for them, and re-layouts: 5.92 us -> 3.6 us
    reduce_sum x3 -> x0, other arithmetic: 2.31 us -> none  [head_block(): probability = exponent / jnp.sum(exponent, axis=-1, keepdims=True)]
  transfers between devices with their start and end apart: 13 -> 15, of which waited for: 8 -> 12; matrix products, arithmetic and copies ran while one was open for 4% -> 0% of each run, Pallas kernels for 0% -> 7%
where the time goes in v2:
time: 82 us; the launch traced here: 81.6 us
  starting transfers between devices  30 us (37%)
  waiting for transfers between devices  27.2 us (33%)
  Pallas kernels  15.4 us (19%)
  other arithmetic  4.52 us (6%)
  local copies, waits for them, and re-layouts  3.72 us (5%)
  between operations  0.84 us (1%)
    ppermute x4, starting transfers between devices, shift(): return lax.ppermute(x, 'ctx', pairs)  15.2 us
    ppermute x4, waiting for transfers between devices, shift(): return lax.ppermute(x, 'ctx', pairs)  14.2 us
    ppermute x9, starting transfers between devices, turn(): return lax.ppermute(x, 'tp', [(i, (i + by) % 4) for i in range(4)])  11.5 us
    ppermute x9, waiting for transfers between devices, turn(): return lax.ppermute(x, 'tp', [(i, (i + by) % 4) for i in range(4)])  8.71 us
    pallas_call x1, Pallas kernels, earlier(): pl.pallas_call(kernel, out_shape=(jax.ShapeDtypeStruct((HEADS, DIM, ROWS)...  7.93 us
    pallas_call x1, Pallas kernels, own_back(): pl.pallas_call(own_back_kernel, out_shape=(jax.ShapeDtypeStruct((HEADS, D...  4.23 us
    ppermute x2, waiting for transfers between devices, swap(): lax.ppermute(x, 'ctx', [(i, i ^ 1) for i in range(lax.axis_size('ctx'))])  4.23 us
    unnamed x20, local copies, waits for them, and re-layouts  3.6 us
  transfers between devices with their start and end apart: 15, of which 12 were waited for; matrix products, arithmetic and copies ran while one was open for 0% of the time, Pallas kernels for 7%

profile of v2, /device:TPU:102, one launch (start us, length us, event | category | flops | bytes accessed | tf_op | source)
XLA Modules:
  0.0 81.6 jit_solution(8365346681790847556)
XLA Ops:
  0.6 0.7 add_convert_fusion.4
  1.3 1.0 %pad_maximum_fusion.2.own_ref = bf16[400,512]{1,0:T(8,128)(2,1)S(1)} fusion(bf16[16,512]{1,0:T(8,128)(2,1)S(1)} %broadcast_in_dim.22.refs_2_, bf16[192,512]{1,0:T(8,128)(2,1)} %bitcast.74, bf16[192,512]{1,0:T(8,128)(2,1)} %bitcast.75), kind=kLoop, calls=%fused_computation.3 | loop fusion | flops 1228800 | bytes 819200 | tf_op jit(solution)/shard_map/concatenate | solution.py:339
  2.4 5.0 %collective-permute-start.4 = (bf16[400,512]{1,0:T(8,128)(2,1)S(1)}, bf16[400,512]{1,0:T(8,128)(2,1)}, u32[]{:S(2)}, u32[]{:S(2)}) collective-permute-start(bf16[400,512]{1,0:T(8,128)(2,1)S(1)} %pad_maximum_fusion.2.own_ref), channel_id=1, source_target_pairs={{0,8},{4,12},{8,16},{12,20},{16,24},{20,28},{24,32},{28,36},{32,40... | collective-permute-start | bytes 1228808 | tf_op jit(solution)/shard_map/ppermute | solution.py:321
  7.4 4.3 %collective-permute-start = (bf16[400,128]{1,0:T(8,128)(2,1)S(1)}, bf16[400,128]{1,0:T(8,128)(2,1)S(1)}, u32[]{:S(2)}, u32[]{:S(2)}) collective-permute-start(bf16[400,128]{1,0:T(8,128)(2,1)S(1)} %constant_dynamic-slice_fusion.4), channel_id=1, source_target_pairs={{0,16},{4,20},{8,24},{12,28},{16,32},{20,36},{24,40},{28,44},{32,4... | collective-permute-start | bytes 307208 | tf_op jit(solution)/shard_map/ppermute | solution.py:321
  11.7 0.0 copy-start.1
  11.7 1.1 %copy-done.1 = bf16[512,3,192]{0,2,1:T(8,128)(2,1)S(1)} copy-done((bf16[512,3,192]{0,2,1:T(8,128)(2,1)S(1)}, bf16[512,3,192]{0,2,1:T(8,128)(2,1)}, u32[]{:S(2)}) %copy-start.1) | copy-done | bytes 589848
  12.8 1.3 %shard_map.84 = (bf16[256,1536]{1,0:T(8,128)(2,1)S(1)}, bf16[1536,192]{1,0:T(8,128)(2,1)S(1)}, bf16[512,1536]{1,0:T(8,128)(2,1)S(1)}, f32[8,1536]{1,0:T(8,128)S(...) custom-call(bf16[3,192,512]{2,1,0:T(8,128)(2,1)S(1)} %bitcast.73, bf16[400,512]{1,0:T(8,128)(2,1)S(1)} %pad_maximum_fusion.2.own_ref), custom_call_target="tpu_custom_call" | custom-call | flops 800000000 | bytes 8000000 | tf_op jit(solution)/shard_map/pallas_call | solution.py:94
  14.1 1.0 %copy-done.2 = f32[192,1536]{1,0:T(8,128)} copy-done((f32[192,1536]{1,0:T(8,128)}, f32[192,1536]{1,0:T(8,128)S(1)}, u32[]{:S(2)}) %copy-start.2) | copy-done | bytes 1179672
  15.2 0.9 %copy-done.4 = bf16[256,1536]{1,0:T(8,128)(2,1)} copy-done((bf16[256,1536]{1,0:T(8,128)(2,1)}, bf16[256,1536]{1,0:T(8,128)(2,1)S(1)}, u32[]{:S(2)}) %copy-start.4) | copy-done | bytes 786456
  16.0 3.7 %collective-permute-done.refs_8_ = bf16[400,128]{1,0:T(8,128)(2,1)S(1)} collective-permute-done((bf16[400,128]{1,0:T(8,128)(2,1)S(1)}, bf16[400,128]{1,0:T(8,128)(2,1)S(1)}, u32[]{:S(2)}, u32[]{:S(2)}) %collective-permute-start) | collective-permute-done | bytes 102432 | tf_op jit(solution)/shard_map/ppermute | solution.py:321
  19.7 3.2 %collective-permute-start.3 = (bf16[400,128]{1,0:T(8,128)(2,1)S(1)}, bf16[400,128]{1,0:T(8,128)(2,1)S(1)}, u32[]{:S(2)}, u32[]{:S(2)}) collective-permute-start(bf16[400,128]{1,0:T(8,128)(2,1)S(1)} %collective-permute-done.refs_8_), channel_id=1, source_target_pairs={{0,2},{1,3},{2,0},{3,1},{4,6},{5,7},{6,4},{7,5},{8,10},{9,11},{10,... | collective-permute-start | bytes 307208 | tf_op jit(solution)/shard_map/ppermute | solution.py:329
  22.9 1.1 %collective-permute-start.2 = (bf16[400,128]{1,0:T(8,128)(2,1)S(1)}, bf16[400,128]{1,0:T(8,128)(2,1)S(1)}, u32[]{:S(2)}, u32[]{:S(2)}) collective-permute-start(bf16[400,128]{1,0:T(8,128)(2,1)S(1)} %collective-permute-done.refs_8_), channel_id=1, source_target_pairs={{0,3},{1,0},{2,1},{3,2},{4,7},{5,4},{6,5},{7,6},{8,11},{9,8},{10,9... | collective-permute-start | bytes 307208 | tf_op jit(solution)/shard_map/ppermute | solution.py:329
  24.0 1.0 %collective-permute-start.1 = (bf16[400,128]{1,0:T(8,128)(2,1)S(1)}, bf16[400,128]{1,0:T(8,128)(2,1)S(1)}, u32[]{:S(2)}, u32[]{:S(2)}) collective-permute-start(bf16[400,128]{1,0:T(8,128)(2,1)S(1)} %collective-permute-done.refs_8_), channel_id=1, source_target_pairs={{0,1},{1,2},{2,3},{3,0},{4,5},{5,6},{6,7},{7,4},{8,9},{9,10},{10,1... | collective-permute-start | bytes 307208 | tf_op jit(solution)/shard_map/ppermute | solution.py:329
  24.9 1.9 %collective-permute-done.3.refs_11_ = bf16[400,128]{1,0:T(8,128)(2,1)S(1)} collective-permute-done((bf16[400,128]{1,0:T(8,128)(2,1)S(1)}, bf16[400,128]{1,0:T(8,128)(2,1)S(1)}, u32[]{:S(2)}, u32[]{:S(2)}) %collective-permute-start.3) | collective-permute-done | bytes 102432 | tf_op jit(solution)/shard_map/ppermute | solution.py:329
  26.9 0.7 collective-permute-done.2.refs_10_
  27.6 2.3 %collective-permute-done.1.refs_9_ = bf16[400,128]{1,0:T(8,128)(2,1)S(1)} collective-permute-done((bf16[400,128]{1,0:T(8,128)(2,1)S(1)}, bf16[400,128]{1,0:T(8,128)(2,1)S(1)}, u32[]{:S(2)}, u32[]{:S(2)}) %collective-permute-start.1) | collective-permute-done | bytes 102432 | tf_op jit(solution)/shard_map/ppermute | solution.py:329
  29.8 0.0 collective-permute-done.4
  29.8 1.2 %select_bitcast_fusion.1 = (bf16[1,400,128]{2,1,0:T(8,128)(2,1)S(1)}, bf16[400,128]{1,0:T(8,128)(2,1)S(1)}, bf16[1,400,128]{2,1,0:T(8,128)(2,1)S(1)}, bf16[400,1...) fusion(bf16[400,128]{1,0:T(8,128)(2,1)S(1)} %collective-permute, ...), kind=kLoop, calls=%fused_computation.25 | loop fusion | flops 204800 | bytes 1638417 | tf_op jit(solution)/shard_map/stack | solution.py:353
  31.1 0.1 select_bitcast_fusion.4
  31.2 0.0 copy-start
  31.3 0.1 pad_maximum_fusion
  31.5 0.1 collective-permute-start.5
  31.6 2.3 %collective-permute-done.5.refs_16_ = bf16[4,2,400,128]{3,2,1,0:T(8,128)(2,1)S(1)} collective-permute-done((bf16[4,2,400,128]{3,2,1,0:T(8,128)(2,1)S(1)}, bf16[4,2,400,128]{3,2,1,0:T(8,128)(2,1)S(1)}, u32[]{:S(2)}, u32[]{:S(2)}) %collective-permute-start.5) | collective-permute-done | bytes 819232 | tf_op jit(solution)/shard_map/ppermute | solution.py:325
  33.9 7.9 %shard_map.85 = (bf16[3,192,512]{2,1,0:T(8,128)(2,1)}, bf16[4,4,128,384]{3,2,1,0:T(8,128)(2,1)S(1)}, bf16[4,512,1536]{2,1,0:T(8,128)(2,1)S(1)}, bf16[4,192,512]{...) custom-call(s32[1]{0:T(128)} %bitcast.refs_0_.tp_ref, bf16[3,192,512]{2,1,0:T(8,128)(2,1)S(1)} %bitcast.71, ...), custom_call_target="tpu_custom_call" | custom-call | flops 8000000000 | bytes 8000000 | tf_op jit(solution)/shard_map/pallas_call | solution.py:211
  41.8 0.1 fusion.10
  41.9 0.1 pad_maximum_fusion.1
  42.0 3.3 %collective-permute-start.6 = (bf16[2,4,128,384]{3,2,1,0:T(8,128)(2,1)S(1)}, bf16[2,4,128,384]{3,2,1,0:T(8,128)(2,1)S(1)}, u32[]{:S(2)}, u32[]{:S(2)}) collective-permute-start(bf16[2,4,128,384]{3,2,1,0:T(8,128)(2,1)S(1)} %pad_maximum_fusion.1), channel_id=1, source_target_pairs={{0,4},{4,0},{8,12},{12,8},{16,20},{20,16},{24,28},{28,24},{32,36},... | collective-permute-start | bytes 2359304 | tf_op jit(solution)/shard_map/ppermute | solution.py:325
  45.3 1.9 %collective-permute-done.6 = bf16[2,4,128,384]{3,2,1,0:T(8,128)(2,1)S(1)} collective-permute-done((bf16[2,4,128,384]{3,2,1,0:T(8,128)(2,1)S(1)}, bf16[2,4,128,384]{3,2,1,0:T(8,128)(2,1)S(1)}, u32[]{:S(2)}, u32[]{:S(2)}) %collective-permute-start.6) | collective-permute-done | bytes 786464 | tf_op jit(solution)/shard_map/ppermute | solution.py:325
  47.2 0.2 fusion
  47.4 4.0 %collective-permute-start.7 = (bf16[4,128,384]{2,1,0:T(8,128)(2,1)S(1)}, bf16[4,128,384]{2,1,0:T(8,128)(2,1)S(1)}, u32[]{:S(2)}, u32[]{:S(2)}) collective-permute-start(bf16[4,128,384]{2,1,0:T(8,128)(2,1)S(1)} %fusion), channel_id=1, source_target_pairs={{8,0},{12,4},{16,8},{20,12},{24,16},{28,20},{32,24},{36,28},{40,32... | collective-permute-start | bytes 1179656 | tf_op jit(solution)/shard_map/ppermute | solution.py:321
  51.4 0.1 fusion.7
  51.5 0.2 collective-permute-start.8
  51.7 1.7 %collective-permute-start.10 = (bf16[128,384]{1,0:T(8,128)(2,1)S(1)}, bf16[128,384]{1,0:T(8,128)(2,1)S(1)}, u32[]{:S(2)}, u32[]{:S(2)}) collective-permute-start(bf16[128,384]{1,0:T(8,128)(2,1)S(1)} %get-tuple-element.59), channel_id=1, source_target_pairs={{0,2},{1,3},{2,0},{3,1},{4,6},{5,7},{6,4},{7,5},{8,10},{9,11},{10,... | collective-permute-start | bytes 294920 | tf_op jit(solution)/shard_map/ppermute | solution.py:329
  53.4 0.2 collective-permute-start.9
  53.6 4.2 %shard_map.86 = (bf16[3,192,512]{2,1,0:T(8,128)(2,1)}, bf16[4,128,384]{2,1,0:T(8,128)(2,1)S(1)}) custom-call(s32[1]{0:T(128)} %bitcast.refs_0_.tp_ref, s32[1]{0:T(128)} %get-tuple-element.40.first_ref, bf16[3,192,512]{2,1,0:T(8,128)(2,1)S(1)} %bitcast.72, bf16[400,512]{1,0:T(8,128)(2,1)S(1)} %pad_maximum_fusion.2.own_ref, ...), custom_call_target="tpu_custom_call" | custom-call | flops 2000000000 | bytes 8000000 | tf_op jit(solution)/shard_map/pallas_call | solution.py:284
  57.8 0.3 collective-permute-done.10
  58.1 1.7 %collective-permute-done.9 = bf16[128,384]{1,0:T(8,128)(2,1)S(1)} collective-permute-done((bf16[128,384]{1,0:T(8,128)(2,1)S(1)}, bf16[128,384]{1,0:T(8,128)(2,1)S(1)}, u32[]{:S(2)}, u32[]{:S(2)}) %collective-permute-start.9) | collective-permute-done | bytes 98336 | tf_op jit(solution)/shard_map/ppermute | solution.py:329
  59.8 4.1 %collective-permute-done.7 = bf16[4,128,384]{2,1,0:T(8,128)(2,1)S(1)} collective-permute-done((bf16[4,128,384]{2,1,0:T(8,128)(2,1)S(1)}, bf16[4,128,384]{2,1,0:T(8,128)(2,1)S(1)}, u32[]{:S(2)}, u32[]{:S(2)}) %collective-permute-start.7) | collective-permute-done | bytes 393248 | tf_op jit(solution)/shard_map/ppermute | solution.py:321
  64.0 0.9 %fusion.1 = (bf16[128,384]{1,0:T(8,128)(2,1)S(1)}, bf16[128,384]{1,0:T(8,128)(2,1)S(1)}, bf16[128,384]{1,0:T(8,128)(2,1)S(1)}, f32[128,384]{1,0:T(8,128)}, bf16[128,384]{1,0:T(8,128)(2,1)S(1)}) fusion(bf16[2,4,128,384]{3,2,1,0:T(8,128)(2,1)S(1)} %collective-permute-done.6, bf16[4,128,384]{2,1,0:T(8,128)(2,1)S(1)} %collective-permute-done.7, ...), kind=kLoop, calls=%fused_computation.11 | loop fusion | flops 1867776 | bytes 2260993 | tf_op jit(solution)/shard_map/convert_element_type | solution.py:372
  64.9 0.9 %collective-permute-start.14 = (bf16[128,384]{1,0:T(8,128)(2,1)S(1)}, bf16[128,384]{1,0:T(8,128)(2,1)S(1)}, u32[]{:S(2)}, u32[]{:S(2)}) collective-permute-start(bf16[128,384]{1,0:T(8,128)(2,1)S(1)} %get-tuple-element.61), channel_id=1, source_target_pairs={{0,2},{1,3},{2,0},{3,1},{4,6},{5,7},{6,4},{7,5},{8,10},{9,11},{10,... | collective-permute-start | bytes 294920 | tf_op jit(solution)/shard_map/ppermute | solution.py:329
  65.8 0.3 collective-permute-start.13
  66.1 2.9 %collective-permute-start.12 = (bf16[128,384]{1,0:T(8,128)(2,1)S(1)}, bf16[128,384]{1,0:T(8,128)(2,1)S(1)}, u32[]{:S(2)}, u32[]{:S(2)}) collective-permute-start(bf16[128,384]{1,0:T(8,128)(2,1)S(1)} %get-tuple-element.63), channel_id=1, source_target_pairs={{0,3},{1,0},{2,1},{3,2},{4,7},{5,4},{6,5},{7,6},{8,11},{9,8},{10,9... | collective-permute-start | bytes 294920 | tf_op jit(solution)/shard_map/ppermute | solution.py:329
  69.0 1.9 %collective-permute-start.11 = (bf16[128,384]{1,0:T(8,128)(2,1)S(1)}, bf16[128,384]{1,0:T(8,128)(2,1)S(1)}, u32[]{:S(2)}, u32[]{:S(2)}) collective-permute-start(bf16[128,384]{1,0:T(8,128)(2,1)S(1)} %get-tuple-element.67), channel_id=1, source_target_pairs={{16,0},{20,4},{24,8},{28,12},{32,16},{36,20},{40,24},{44,28},{48,3... | collective-permute-start | bytes 294920 | tf_op jit(solution)/shard_map/ppermute | solution.py:321
  70.9 0.8 collective-permute-done.14.refs_4_
  71.7 1.0 %collective-permute-done.13.refs_3_ = bf16[128,384]{1,0:T(8,128)(2,1)S(1)} collective-permute-done((bf16[128,384]{1,0:T(8,128)(2,1)S(1)}, bf16[128,384]{1,0:T(8,128)(2,1)S(1)}, u32[]{:S(2)}, u32[]{:S(2)}) %collective-permute-start.13) | collective-permute-done | bytes 98336 | tf_op jit(solution)/shard_map/ppermute | solution.py:329
  72.7 6.4 %collective-permute-done.11.refs_1_ = bf16[128,384]{1,0:T(8,128)(2,1)S(1)} collective-permute-done((bf16[128,384]{1,0:T(8,128)(2,1)S(1)}, bf16[128,384]{1,0:T(8,128)(2,1)S(1)}, u32[]{:S(2)}, u32[]{:S(2)}) %collective-permute-start.11) | collective-permute-done | bytes 98336 | tf_op jit(solution)/shard_map/ppermute | solution.py:321
  79.1 0.6 copy-done.9
  79.8 1.9 %shard_map.87 = (bf16[192,128]{1,0:T(8,128)(2,1)}, bf16[192,128]{1,0:T(8,128)(2,1)}) custom-call(f32[128,384]{1,0:T(8,128)} %get-tuple-element.64.refs_0_, bf16[128,384]{1,0:T(8,128)(2,1)} %copy-done.9, bf16[128,384]{1,0:T(8,128)(2,1)} %copy-done.8, bf16[128,384]{1,0:T(8,128)(2,1)} %copy-done.7, bf16[128,384]{1,0:T(8,128)(2,1)} %copy-done.6), custom_call_target="tpu_custom_call" | custom-call | tf_op jit(solution)/shard_map/pallas_call | solution.py:313
  (22 shorter events, 0.1 us)
Async XLA Ops:
  2.4 27.5 %collective-permute-start.4 = (bf16[400,512]{1,0:T(8,128)(2,1)S(1)}, bf16[400,512]{1,0:T(8,128)(2,1)}, u32[]{:S(2)}, u32[]{:S(2)}) collective-permute-start(bf16[400,512]{1,0:T(8,128)(2,1)S(1)} %pad_maximum_fusion.2.own_ref), channel_id=1, source_target_pairs={{0,8},{4,12},{8,16},{12,20},{16,24},{20,28},{24,32},{28,36},{32,40... | collective-permute-start | bytes 1228808 | tf_op jit(solution)/shard_map/ppermute | solution.py:321
  7.4 12.3 %collective-permute-start = (bf16[400,128]{1,0:T(8,128)(2,1)S(1)}, bf16[400,128]{1,0:T(8,128)(2,1)S(1)}, u32[]{:S(2)}, u32[]{:S(2)}) collective-permute-start(bf16[400,128]{1,0:T(8,128)(2,1)S(1)} %constant_dynamic-slice_fusion.4), channel_id=1, source_target_pairs={{0,16},{4,20},{8,24},{12,28},{16,32},{20,36},{24,40},{28,44},{32,4... | collective-permute-start | bytes 307208 | tf_op jit(solution)/shard_map/ppermute | solution.py:321
  11.7 1.1 %copy-start.1 = (bf16[512,3,192]{0,2,1:T(8,128)(2,1)S(1)}, bf16[512,3,192]{0,2,1:T(8,128)(2,1)}, u32[]{:S(2)}) copy-start(bf16[512,3,192]{0,2,1:T(8,128)(2,1)} %param.5) | copy-start | bytes 1769476
  14.1 1.0 %copy-start.2 = (f32[192,1536]{1,0:T(8,128)}, f32[192,1536]{1,0:T(8,128)S(1)}, u32[]{:S(2)}) copy-start(f32[192,1536]{1,0:T(8,128)S(1)} %get-tuple-element.37.refs_7_) | copy-start | bytes 3538948
  15.2 0.9 %copy-start.4 = (bf16[256,1536]{1,0:T(8,128)(2,1)}, bf16[256,1536]{1,0:T(8,128)(2,1)S(1)}, u32[]{:S(2)}) copy-start(bf16[256,1536]{1,0:T(8,128)(2,1)S(1)} %get-tuple-element.33.refs_3_) | copy-start | bytes 2359300
  19.7 7.1 %collective-permute-start.3 = (bf16[400,128]{1,0:T(8,128)(2,1)S(1)}, bf16[400,128]{1,0:T(8,128)(2,1)S(1)}, u32[]{:S(2)}, u32[]{:S(2)}) collective-permute-start(bf16[400,128]{1,0:T(8,128)(2,1)S(1)} %collective-permute-done.refs_8_), channel_id=1, source_target_pairs={{0,2},{1,3},{2,0},{3,1},{4,6},{5,7},{6,4},{7,5},{8,10},{9,11},{10,... | collective-permute-start | bytes 307208 | tf_op jit(solution)/shard_map/ppermute | solution.py:329
  22.9 4.7 %collective-permute-start.2 = (bf16[400,128]{1,0:T(8,128)(2,1)S(1)}, bf16[400,128]{1,0:T(8,128)(2,1)S(1)}, u32[]{:S(2)}, u32[]{:S(2)}) collective-permute-start(bf16[400,128]{1,0:T(8,128)(2,1)S(1)} %collective-permute-done.refs_8_), channel_id=1, source_target_pairs={{0,3},{1,0},{2,1},{3,2},{4,7},{5,4},{6,5},{7,6},{8,11},{9,8},{10,9... | collective-permute-start | bytes 307208 | tf_op jit(solution)/shard_map/ppermute | solution.py:329
  24.0 5.9 %collective-permute-start.1 = (bf16[400,128]{1,0:T(8,128)(2,1)S(1)}, bf16[400,128]{1,0:T(8,128)(2,1)S(1)}, u32[]{:S(2)}, u32[]{:S(2)}) collective-permute-start(bf16[400,128]{1,0:T(8,128)(2,1)S(1)} %collective-permute-done.refs_8_), channel_id=1, source_target_pairs={{0,1},{1,2},{2,3},{3,0},{4,5},{5,6},{6,7},{7,4},{8,9},{9,10},{10,1... | collective-permute-start | bytes 307208 | tf_op jit(solution)/shard_map/ppermute | solution.py:329
  31.2 2.7 %copy-start = (bf16[512,3,192]{0,2,1:T(8,128)(2,1)S(1)}, bf16[512,3,192]{0,2,1:T(8,128)(2,1)}, u32[]{:S(2)}) copy-start(bf16[512,3,192]{0,2,1:T(8,128)(2,1)} %param.8) | copy-start | bytes 1769476
  31.2 2.7 %copy-start.3 = (f32[192,1536]{1,0:T(8,128)S(1)}, f32[192,1536]{1,0:T(8,128)}, u32[]{:S(2)}) copy-start(f32[192,1536]{1,0:T(8,128)} %copy-done.2) | copy-start | bytes 3538948
  31.2 2.7 %copy-start.5 = (bf16[256,1536]{1,0:T(8,128)(2,1)S(1)}, bf16[256,1536]{1,0:T(8,128)(2,1)}, u32[]{:S(2)}) copy-start(bf16[256,1536]{1,0:T(8,128)(2,1)} %copy-done.4) | copy-start | bytes 2359300
  31.5 2.4 %collective-permute-start.5 = (bf16[4,2,400,128]{3,2,1,0:T(8,128)(2,1)S(1)}, bf16[4,2,400,128]{3,2,1,0:T(8,128)(2,1)S(1)}, u32[]{:S(2)}, u32[]{:S(2)}) collective-permute-start(bf16[4,2,400,128]{3,2,1,0:T(8,128)(2,1)S(1)} %pad_maximum_fusion), channel_id=1, source_target_pairs={{0,4},{4,0},{8,12},{12,8},{16,20},{20,16},{24,28},{28,24},{32,36},... | collective-permute-start | bytes 2457608 | tf_op jit(solution)/shard_map/ppermute | solution.py:325
  42.0 5.2 %collective-permute-start.6 = (bf16[2,4,128,384]{3,2,1,0:T(8,128)(2,1)S(1)}, bf16[2,4,128,384]{3,2,1,0:T(8,128)(2,1)S(1)}, u32[]{:S(2)}, u32[]{:S(2)}) collective-permute-start(bf16[2,4,128,384]{3,2,1,0:T(8,128)(2,1)S(1)} %pad_maximum_fusion.1), channel_id=1, source_target_pairs={{0,4},{4,0},{8,12},{12,8},{16,20},{20,16},{24,28},{28,24},{32,36},... | collective-permute-start | bytes 2359304 | tf_op jit(solution)/shard_map/ppermute | solution.py:325
  47.4 16.6 %collective-permute-start.7 = (bf16[4,128,384]{2,1,0:T(8,128)(2,1)S(1)}, bf16[4,128,384]{2,1,0:T(8,128)(2,1)S(1)}, u32[]{:S(2)}, u32[]{:S(2)}) collective-permute-start(bf16[4,128,384]{2,1,0:T(8,128)(2,1)S(1)} %fusion), channel_id=1, source_target_pairs={{8,0},{12,4},{16,8},{20,12},{24,16},{28,20},{32,24},{36,28},{40,32... | collective-permute-start | bytes 1179656 | tf_op jit(solution)/shard_map/ppermute | solution.py:321
  51.5 6.3 %collective-permute-start.8 = (bf16[128,384]{1,0:T(8,128)(2,1)S(1)}, bf16[128,384]{1,0:T(8,128)(2,1)S(1)}, u32[]{:S(2)}, u32[]{:S(2)}) collective-permute-start(bf16[128,384]{1,0:T(8,128)(2,1)S(1)} %get-tuple-element.58), channel_id=1, source_target_pairs={{0,3},{1,0},{2,1},{3,2},{4,7},{5,4},{6,5},{7,6},{8,11},{9,8},{10,9... | collective-permute-start | bytes 294920 | tf_op jit(solution)/shard_map/ppermute | solution.py:329
  51.7 6.4 %collective-permute-start.10 = (bf16[128,384]{1,0:T(8,128)(2,1)S(1)}, bf16[128,384]{1,0:T(8,128)(2,1)S(1)}, u32[]{:S(2)}, u32[]{:S(2)}) collective-permute-start(bf16[128,384]{1,0:T(8,128)(2,1)S(1)} %get-tuple-element.59), channel_id=1, source_target_pairs={{0,2},{1,3},{2,0},{3,1},{4,6},{5,7},{6,4},{7,5},{8,10},{9,11},{10,... | collective-permute-start | bytes 294920 | tf_op jit(solution)/shard_map/ppermute | solution.py:329
  53.4 6.4 %collective-permute-start.9 = (bf16[128,384]{1,0:T(8,128)(2,1)S(1)}, bf16[128,384]{1,0:T(8,128)(2,1)S(1)}, u32[]{:S(2)}, u32[]{:S(2)}) collective-permute-start(bf16[128,384]{1,0:T(8,128)(2,1)S(1)} %get-tuple-element.60), channel_id=1, source_target_pairs={{0,1},{1,2},{2,3},{3,0},{4,5},{5,6},{6,7},{7,4},{8,9},{9,10},{10,1... | collective-permute-start | bytes 294920 | tf_op jit(solution)/shard_map/ppermute | solution.py:329
  64.9 6.9 %collective-permute-start.14 = (bf16[128,384]{1,0:T(8,128)(2,1)S(1)}, bf16[128,384]{1,0:T(8,128)(2,1)S(1)}, u32[]{:S(2)}, u32[]{:S(2)}) collective-permute-start(bf16[128,384]{1,0:T(8,128)(2,1)S(1)} %get-tuple-element.61), channel_id=1, source_target_pairs={{0,2},{1,3},{2,0},{3,1},{4,6},{5,7},{6,4},{7,5},{8,10},{9,11},{10,... | collective-permute-start | bytes 294920 | tf_op jit(solution)/shard_map/ppermute | solution.py:329
  65.8 7.0 %collective-permute-start.13 = (bf16[128,384]{1,0:T(8,128)(2,1)S(1)}, bf16[128,384]{1,0:T(8,128)(2,1)S(1)}, u32[]{:S(2)}, u32[]{:S(2)}) collective-permute-start(bf16[128,384]{1,0:T(8,128)(2,1)S(1)} %get-tuple-element.62), channel_id=1, source_target_pairs={{0,1},{1,2},{2,3},{3,0},{4,5},{5,6},{6,7},{7,4},{8,9},{9,10},{10,1... | collective-permute-start | bytes 294920 | tf_op jit(solution)/shard_map/ppermute | solution.py:329
  66.1 6.7 %collective-permute-start.12 = (bf16[128,384]{1,0:T(8,128)(2,1)S(1)}, bf16[128,384]{1,0:T(8,128)(2,1)S(1)}, u32[]{:S(2)}, u32[]{:S(2)}) collective-permute-start(bf16[128,384]{1,0:T(8,128)(2,1)S(1)} %get-tuple-element.63), channel_id=1, source_target_pairs={{0,3},{1,0},{2,1},{3,2},{4,7},{5,4},{6,5},{7,6},{8,11},{9,8},{10,9... | collective-permute-start | bytes 294920 | tf_op jit(solution)/shard_map/ppermute | solution.py:329
  69.0 10.1 %collective-permute-start.11 = (bf16[128,384]{1,0:T(8,128)(2,1)S(1)}, bf16[128,384]{1,0:T(8,128)(2,1)S(1)}, u32[]{:S(2)}, u32[]{:S(2)}) collective-permute-start(bf16[128,384]{1,0:T(8,128)(2,1)S(1)} %get-tuple-element.67), channel_id=1, source_target_pairs={{16,0},{20,4},{24,8},{28,12},{32,16},{36,20},{40,24},{44,28},{48,3... | collective-permute-start | bytes 294920 | tf_op jit(solution)/shard_map/ppermute | solution.py:321
  71.7 7.4 %copy-start.6 = (bf16[128,384]{1,0:T(8,128)(2,1)}, bf16[128,384]{1,0:T(8,128)(2,1)S(1)}, u32[]{:S(2)}) copy-start(bf16[128,384]{1,0:T(8,128)(2,1)S(1)} %collective-permute-done.14.refs_4_) | copy-start | bytes 294916
  72.7 6.4 %copy-start.7 = (bf16[128,384]{1,0:T(8,128)(2,1)}, bf16[128,384]{1,0:T(8,128)(2,1)S(1)}, u32[]{:S(2)}) copy-start(bf16[128,384]{1,0:T(8,128)(2,1)S(1)} %collective-permute-done.13.refs_3_) | copy-start | bytes 294916
  72.7 6.4 %copy-start.8 = (bf16[128,384]{1,0:T(8,128)(2,1)}, bf16[128,384]{1,0:T(8,128)(2,1)S(1)}, u32[]{:S(2)}) copy-start(bf16[128,384]{1,0:T(8,128)(2,1)S(1)} %collective-permute-done.12.refs_2_) | copy-start | bytes 294916
  79.1 0.6 copy-start.9
